TPU v7x, 32 devices: a whole 2x2x4 slice. The times are simulated.
32 devices in a mesh: rows: 4 (over y, core), mp: 8 (over z, x).
Axes of the slice: x: 2, y: 2, z: 4, core: 2. Of those that a mesh axis runs over, the one named last changes fastest.
Arguments:
- tokens: bfloat16 [8192, 1024], P(('rows', 'mp')), may hold values from -6 to 6
- segment_ids: int32 [8192], P('rows'), may hold values from 0 to 3, as said below
- cotangent: bfloat16 [8192, 1024], P(('rows', 'mp')), may hold values from -6 to 6
- ln_attn_gain: float32 [2, 1024], replicated, may hold values from 0.25 to 1.75
- ln_attn_bias: float32 [2, 1024], replicated, may hold values from -4 to 4
- qkv_weight: bfloat16 [2, 1024, 3, 1024], P(None, None, None, 'mp'), may hold values from -0.1875 to 0.1875
- qv_bias: float32 [2, 2, 1024], P(None, None, 'mp'), may hold values from -4 to 4
- head_scale: float32 [2, 16], replicated, may hold values from 0.25 to 1.75
- out_weight: bfloat16 [2, 1024, 1024], P(None, 'mp'), may hold values from -0.1875 to 0.1875
- out_bias: float32 [2, 1024], replicated, may hold values from -4 to 4
- ln_post_gain: float32 [2, 1024], replicated, may hold values from 0.25 to 1.75
- ln_post_bias: float32 [2, 1024], replicated, may hold values from -4 to 4
- ln_ffn_gain: float32 [2, 1024], replicated, may hold values from 0.25 to 1.75
- ln_ffn_bias: float32 [2, 1024], replicated, may hold values from -4 to 4
- fc1_weight: bfloat16 [2, 1024, 4096], P(None, None, 'mp'), may hold values from -0.1875 to 0.1875
- fc1_bias: float32 [2, 4096], P(None, 'mp'), may hold values from -4 to 4
- mid_gain: float32 [2, 4096], P(None, 'mp'), may hold values from 0.25 to 1.75
- mid_bias: float32 [2, 4096], P(None, 'mp'), may hold values from -4 to 4
- fc2_weight: bfloat16 [2, 4096, 1024], P(None, 'mp'), may hold values from -0.09375 to 0.09375
- fc2_bias: float32 [2, 1024], replicated, may hold values from -4 to 4
Outputs:
- layer_output: bfloat16 [8192, 1024], P(('rows', 'mp'))
- input_grad: float32 [8192, 1024], P(('rows', 'mp'))
- ln_attn_gain_grad: float32 [2, 1024], replicated
- ln_attn_bias_grad: float32 [2, 1024], replicated
- qkv_weight_grad: float32 [2, 1024, 3, 1024], P(None, None, None, 'mp')
- qv_bias_grad: float32 [2, 2, 1024], P(None, None, 'mp')
- head_scale_grad: float32 [2, 16], replicated
- out_weight_grad: float32 [2, 1024, 1024], P(None, 'mp')
- out_bias_grad: float32 [2, 1024], replicated
- ln_post_gain_grad: float32 [2, 1024], replicated
- ln_post_bias_grad: float32 [2, 1024], replicated
- ln_ffn_gain_grad: float32 [2, 1024], replicated
- ln_ffn_bias_grad: float32 [2, 1024], replicated
- fc1_weight_grad: float32 [2, 1024, 4096], P(None, None, 'mp')
- fc1_bias_grad: float32 [2, 4096], P(None, 'mp')
- mid_gain_grad: float32 [2, 4096], P(None, 'mp')
- mid_bias_grad: float32 [2, 4096], P(None, 'mp')
- fc2_weight_grad: float32 [2, 4096, 1024], P(None, 'mp')
- fc2_bias_grad: float32 [2, 1024], replicated
Inputs may be any that keep to these rules, and one draw needn't show every extreme that they name: `segment_ids`: ids restart at 0 in every aligned group of 2048 tokens and never fall within it; in each group document 0 holds more than 1792 tokens and documents 1 to 3 lie in the group's last 256 tokens.
All inputs are finite; a program needn't handle non-finite values.
Results may differ from a plain program's by a relative error of at most 0.022.
Values may be sent and summed in bfloat16 or wider, within the bound.
A program may use at most 256 MiB of HBM per device.

v0:
```python
from functools import partial

import jax
import jax.numpy as jnp
from jax import lax
from jax.sharding import PartitionSpec as P

epsilon = 1e-05
masked = -1e30


def partner(shard, axis, stride):
    return lax.ppermute(shard, axis, [(i, i ^ 1 << stride) for i in range(lax.axis_size(axis))])


def norm_local(values, gain_row, bias_row):
    average = jnp.mean(values, axis=-1, keepdims=True)
    centered = values - average
    spread = jnp.mean(centered * centered, axis=-1, keepdims=True)
    factor = lax.rsqrt(spread + epsilon)
    normal = centered * factor
    return (normal * gain_row + bias_row, normal, factor)


def norm_back(grad_out, normal, factor, gain_row):
    scaled = grad_out * gain_row
    inner_sum = jnp.mean(scaled * normal, axis=-1, keepdims=True)
    return factor * (scaled - jnp.mean(scaled, axis=-1, keepdims=True) - normal * inner_sum)


def collect_rows(normed_b):
    return lax.all_gather(normed_b, "mp", axis=0, tiled=True)


def collect_grads(gradient_b):
    return lax.all_gather(gradient_b, "mp", axis=0, tiled=True)


def reduce_branch(operand_b, weight_b, local_rows):

    def partial_term(first_row, count):
        return jnp.dot(operand_b, weight_b, preferred_element_type=jnp.float32)

    return lax.psum_scatter(
        partial_term(jnp.int32(0), local_rows * lax.axis_size("mp")).astype(jnp.bfloat16),
        "mp",
        scatter_dimension=0,
        tiled=True,
    ).astype(jnp.float32)


def reduce_grads(operand_b, weight_b, local_rows):

    def partial_term(first_row, count):
        return jnp.einsum("tc,dc->td", operand_b, weight_b, preferred_element_type=jnp.float32)

    return lax.psum_scatter(
        partial_term(jnp.int32(0), local_rows * lax.axis_size("mp")).astype(jnp.bfloat16),
        "mp",
        scatter_dimension=0,
        tiled=True,
    ).astype(jnp.float32)


def hidden_stats(first_sum, second_sum):
    return lax.psum((first_sum, second_sum), "mp")


def hidden_grad_stats(first_sum, second_sum):
    return lax.psum((first_sum, second_sum), "mp")


def join_cols(mine, other, is_upper):
    lower_part = jnp.where(is_upper, other, mine)
    upper_part = jnp.where(is_upper, mine, other)
    return jnp.concatenate([lower_part, upper_part], axis=-1)


def join_rows(mine, other, is_upper):
    lower_part = jnp.where(is_upper, other, mine)
    upper_part = jnp.where(is_upper, mine, other)
    return jnp.concatenate([lower_part, upper_part], axis=0)


def split_cols(values, cols_here, is_upper):
    lower_part = values[..., :cols_here]
    upper_part = values[..., cols_here:]
    return (
        jnp.where(is_upper, upper_part, lower_part),
        jnp.where(is_upper, lower_part, upper_part),
    )


def masked_scores(query_block, key_rows, query_start, block_rows, doc_rows, positions):
    factor = query_block.shape[-1] ** (-0.5)
    scores = (
        jnp.einsum("qhe,khe->hqk", query_block, key_rows, preferred_element_type=jnp.float32)
        * factor
    )
    query_place = query_start + jnp.arange(block_rows, dtype=jnp.int32)
    query_docs = lax.dynamic_slice_in_dim(doc_rows, query_start, block_rows, 0)
    allowed = (query_docs[:, None] == doc_rows[None, :]) & (
        query_place[:, None] >= positions[None, :]
    )
    return jnp.where(allowed[None], scores, masked)


def attend_forward(queries, key_rows, value_rows, doc_rows, row_offset):
    total_rows = queries.shape[0]
    block_rows = min(512, total_rows)
    positions = jnp.arange(key_rows.shape[0], dtype=jnp.int32)

    def one_block(first_row):
        query_block = lax.dynamic_slice_in_dim(queries, first_row, block_rows, 0)
        scores = masked_scores(
            query_block, key_rows, row_offset + first_row, block_rows, doc_rows, positions
        )
        row_peak = jnp.max(scores, axis=-1, keepdims=True)
        weights = jnp.exp(scores - row_peak)
        totals = jnp.sum(weights, axis=-1, keepdims=True)
        probabilities = (weights / totals).astype(jnp.bfloat16)
        output = jnp.einsum(
            "hqk,khe->qhe", probabilities, value_rows, preferred_element_type=jnp.float32
        )
        return (output, (row_peak + jnp.log(totals))[..., 0])

    starts = jnp.arange(total_rows // block_rows, dtype=jnp.int32) * block_rows
    outputs, log_totals = lax.map(one_block, starts)
    return (outputs.reshape(queries.shape), log_totals)


def attend_backward(queries, key_rows, value_rows, doc_rows, row_offset, log_totals, grad_out):
    total_rows = queries.shape[0]
    block_rows = min(512, total_rows)
    positions = jnp.arange(key_rows.shape[0], dtype=jnp.int32)
    factor = queries.shape[-1] ** (-0.5)

    def one_block(running, first_row):
        key_grad, value_grad = running
        query_block = lax.dynamic_slice_in_dim(queries, first_row, block_rows, 0)
        grad_block = lax.dynamic_slice_in_dim(grad_out, first_row, block_rows, 0)
        scores = masked_scores(
            query_block, key_rows, row_offset + first_row, block_rows, doc_rows, positions
        )
        block_totals = lax.dynamic_index_in_dim(
            log_totals, first_row // block_rows, 0, keepdims=False
        )
        probabilities = jnp.exp(scores - block_totals[..., None])
        prob_grad = jnp.einsum(
            "qhe,khe->hqk", grad_block, value_rows, preferred_element_type=jnp.float32
        )
        inner_sum = jnp.sum(probabilities * prob_grad, axis=-1, keepdims=True)
        score_grad = (probabilities * (prob_grad - inner_sum)).astype(jnp.bfloat16)
        query_grad = (
            jnp.einsum("hqk,khe->qhe", score_grad, key_rows, preferred_element_type=jnp.float32)
            * factor
        )
        key_grad = (
            key_grad
            + jnp.einsum(
                "hqk,qhe->khe", score_grad, query_block, preferred_element_type=jnp.float32
            )
            * factor
        )
        value_grad = value_grad + jnp.einsum(
            "hqk,qhe->khe",
            probabilities.astype(jnp.bfloat16),
            grad_block,
            preferred_element_type=jnp.float32,
        )
        return ((key_grad, value_grad), query_grad)

    starts = jnp.arange(total_rows // block_rows, dtype=jnp.int32) * block_rows
    zero_grads = jnp.zeros(key_rows.shape, jnp.float32)
    (key_grad, value_grad), query_grads = lax.scan(one_block, (zero_grads, zero_grads), starts)
    return (query_grads.reshape(queries.shape), key_grad, value_grad)


def stack_layers(layer_list, members):
    stacked = []
    for member_index in range(members):
        stacked.append(jnp.stack([entry[member_index] for entry in layer_list], axis=0))
    return stacked


def per_device(
    tokens,
    segment_ids,
    cotangent,
    ln_attn_gain,
    ln_attn_bias,
    qkv_weight,
    qv_bias,
    head_scale,
    out_weight,
    out_bias,
    ln_post_gain,
    ln_post_bias,
    ln_ffn_gain,
    ln_ffn_bias,
    fc1_weight,
    fc1_bias,
    mid_gain,
    mid_bias,
    fc2_weight,
    fc2_bias,
):
    layers = qkv_weight.shape[0]
    local_rows = tokens.shape[0]
    model_width = tokens.shape[1]
    cols_here = qkv_weight.shape[3]
    heads_all = head_scale.shape[1]
    head_width = model_width // heads_all
    pair_cols = 2 * cols_here
    pair_heads = pair_cols // head_width
    group_rows = segment_ids.shape[0]
    half_rows = group_rows // 2
    hidden_all = fc1_weight.shape[2] * lax.axis_size("mp")
    device_index = lax.axis_index("mp")
    is_upper = device_index % 2 == 1
    own_start = jnp.where(is_upper, half_rows, 0).astype(jnp.int32)
    other_start = jnp.where(is_upper, 0, half_rows).astype(jnp.int32)
    first_head = device_index // 2 * pair_heads
    pair_onehot = (
        (first_head + jnp.arange(pair_heads, dtype=jnp.int32))[:, None]
        == jnp.arange(heads_all, dtype=jnp.int32)[None, :]
    ).astype(jnp.float32)
    residual = tokens.astype(jnp.float32)
    stored = []
    for layer_index in range(layers):
        attn_in, attn_normal, attn_factor = norm_local(
            residual, ln_attn_gain[layer_index], ln_attn_bias[layer_index]
        )
        attn_rows = collect_rows(attn_in.astype(jnp.bfloat16))
        qkv_here = qkv_weight[layer_index].reshape(model_width, 3 * cols_here)
        projected = jnp.dot(attn_rows, qkv_here, preferred_element_type=jnp.float32).reshape(
            -1, 3, cols_here
        )
        bias_pair = qv_bias[layer_index]
        query_mine = (projected[:, 0] + bias_pair[0]).astype(jnp.bfloat16)
        key_mine = projected[:, 1].astype(jnp.bfloat16)
        value_mine = (projected[:, 2] + bias_pair[1]).astype(jnp.bfloat16)
        query_send = lax.dynamic_slice_in_dim(query_mine, other_start, half_rows, 0)
        query_recv, key_recv, value_recv = partner((query_send, key_mine, value_mine), "mp", 0)
        query_own = lax.dynamic_slice_in_dim(query_mine, own_start, half_rows, 0)
        queries = join_cols(query_own, query_recv, is_upper).reshape(
            half_rows, pair_heads, head_width
        )
        key_rows = join_cols(key_mine, key_recv, is_upper).reshape(
            group_rows, pair_heads, head_width
        )
        value_rows = join_cols(value_mine, value_recv, is_upper).reshape(
            group_rows, pair_heads, head_width
        )
        attended, log_totals = attend_forward(queries, key_rows, value_rows, segment_ids, own_start)
        pair_scale = jnp.sum(pair_onehot * head_scale[layer_index][None, :], axis=1)
        scaled_half = (
            (attended * pair_scale[None, :, None])
            .astype(jnp.bfloat16)
            .reshape(half_rows, pair_cols)
        )
        own_cols, other_cols = split_cols(scaled_half, cols_here, is_upper)
        scaled_recv = partner(other_cols, "mp", 0)
        scaled_mine = join_rows(own_cols, scaled_recv, is_upper)
        branch = (
            reduce_branch(scaled_mine, out_weight[layer_index], local_rows) + out_bias[layer_index]
        )
        post_out, post_normal, post_factor = norm_local(
            branch, ln_post_gain[layer_index], ln_post_bias[layer_index]
        )
        middle = residual + post_out
        ffn_in, ffn_normal, ffn_factor = norm_local(
            middle, ln_ffn_gain[layer_index], ln_ffn_bias[layer_index]
        )
        ffn_rows = collect_rows(ffn_in.astype(jnp.bfloat16))
        before_gelu = (
            jnp.dot(ffn_rows, fc1_weight[layer_index], preferred_element_type=jnp.float32)
            + fc1_bias[layer_index]
        )
        activated = jax.nn.gelu(before_gelu, approximate=False)
        first_sum, second_sum = hidden_stats(
            jnp.sum(activated, axis=1), jnp.sum(activated * activated, axis=1)
        )
        average = first_sum / hidden_all
        spread = second_sum / hidden_all - average * average
        hidden_factor = lax.rsqrt(spread + epsilon)[:, None]
        hidden_normal = (activated - average[:, None]) * hidden_factor
        mixed_b = (hidden_normal * mid_gain[layer_index] + mid_bias[layer_index]).astype(
            jnp.bfloat16
        )
        ffn_out = reduce_branch(mixed_b, fc2_weight[layer_index], local_rows)
        stored.append(
            (
                attn_normal,
                attn_factor,
                attn_rows,
                queries,
                key_rows,
                value_rows,
                attended,
                log_totals,
                pair_scale,
                scaled_mine,
                post_normal,
                post_factor,
                ffn_normal,
                ffn_factor,
                ffn_rows,
                before_gelu,
                hidden_normal,
                hidden_factor,
                mixed_b,
            )
        )
        residual = middle + ffn_out + fc2_bias[layer_index]
    layer_output = residual.astype(jnp.bfloat16)
    gradient = cotangent.astype(jnp.float32)
    sharded_list = []
    shared_list = []
    for layer_index in reversed(range(layers)):
        (
            attn_normal,
            attn_factor,
            attn_rows,
            queries,
            key_rows,
            value_rows,
            attended,
            log_totals,
            pair_scale,
            scaled_mine,
            post_normal,
            post_factor,
            ffn_normal,
            ffn_factor,
            ffn_rows,
            before_gelu,
            hidden_normal,
            hidden_factor,
            mixed_b,
        ) = stored[layer_index]
        qkv_here = qkv_weight[layer_index].reshape(model_width, 3 * cols_here)
        second_shift_grad = jnp.sum(gradient, axis=0)
        grad_rows = collect_grads(gradient.astype(jnp.bfloat16))
        mixed_grad = jnp.einsum(
            "td,fd->tf", grad_rows, fc2_weight[layer_index], preferred_element_type=jnp.float32
        )
        second_grad = jnp.einsum(
            "tf,td->fd", mixed_b, grad_rows, preferred_element_type=jnp.float32
        )
        hidden_gain_grad = jnp.sum(mixed_grad * hidden_normal, axis=0)
        hidden_shift_grad = jnp.sum(mixed_grad, axis=0)
        normal_grad = mixed_grad * mid_gain[layer_index]
        grad_first, grad_second = hidden_grad_stats(
            jnp.sum(normal_grad, axis=1), jnp.sum(normal_grad * hidden_normal, axis=1)
        )
        active_grad = hidden_factor * (
            normal_grad
            - grad_first[:, None] / hidden_all
            - hidden_normal * grad_second[:, None] / hidden_all
        )
        gelu_pull = jax.vjp(partial(jax.nn.gelu, approximate=False), before_gelu)[1]
        pre_grad_b = gelu_pull(active_grad)[0].astype(jnp.bfloat16)
        first_shift_grad = jnp.sum(pre_grad_b, axis=0, dtype=jnp.float32)
        first_grad = jnp.einsum(
            "td,tf->df", ffn_rows, pre_grad_b, preferred_element_type=jnp.float32
        )
        ffn_in_grad = reduce_grads(pre_grad_b, fc1_weight[layer_index], local_rows)
        ffn_gain_grad = jnp.sum(ffn_in_grad * ffn_normal, axis=0)
        ffn_bias_grad = jnp.sum(ffn_in_grad, axis=0)
        middle_grad = gradient + norm_back(
            ffn_in_grad, ffn_normal, ffn_factor, ln_ffn_gain[layer_index]
        )
        post_gain_grad = jnp.sum(middle_grad * post_normal, axis=0)
        post_bias_grad = jnp.sum(middle_grad, axis=0)
        branch_grad = norm_back(middle_grad, post_normal, post_factor, ln_post_gain[layer_index])
        out_shift_grad = jnp.sum(branch_grad, axis=0)
        branch_rows = collect_grads(branch_grad.astype(jnp.bfloat16))
        scaled_grad = jnp.einsum(
            "td,cd->tc", branch_rows, out_weight[layer_index], preferred_element_type=jnp.float32
        )
        out_grad = jnp.einsum(
            "tc,td->cd", scaled_mine, branch_rows, preferred_element_type=jnp.float32
        )
        grad_send = lax.dynamic_slice_in_dim(scaled_grad, other_start, half_rows, 0)
        grad_recv = partner(grad_send.astype(jnp.bfloat16), "mp", 0).astype(grad_send.dtype)
        grad_own = lax.dynamic_slice_in_dim(scaled_grad, own_start, half_rows, 0)
        scaled_pair = join_cols(grad_own, grad_recv, is_upper).reshape(
            half_rows, pair_heads, head_width
        )
        pair_scale_grad = jnp.sum(attended * scaled_pair, axis=(0, 2))
        scale_grad = jnp.sum(pair_onehot * pair_scale_grad[:, None], axis=0)
        attended_grad_b = (scaled_pair * pair_scale[None, :, None]).astype(jnp.bfloat16)
        query_grad, key_grad, value_grad = attend_backward(
            queries, key_rows, value_rows, segment_ids, own_start, log_totals, attended_grad_b
        )
        query_own, query_other = split_cols(
            query_grad.reshape(half_rows, pair_cols), cols_here, is_upper
        )
        key_own, key_other = split_cols(
            key_grad.reshape(group_rows, pair_cols), cols_here, is_upper
        )
        value_own, value_other = split_cols(
            value_grad.reshape(group_rows, pair_cols), cols_here, is_upper
        )
        query_recv, key_recv, value_recv = (
            partner(query_other.astype(jnp.bfloat16), "mp", 0).astype(query_other.dtype),
            partner(key_other.astype(jnp.bfloat16), "mp", 0).astype(key_other.dtype),
            partner(value_other.astype(jnp.bfloat16), "mp", 0).astype(value_other.dtype),
        )
        query_grad_b = join_rows(query_own, query_recv, is_upper).astype(jnp.bfloat16)
        key_grad_b = (key_own + key_recv).astype(jnp.bfloat16)
        value_grad_b = (value_own + value_recv).astype(jnp.bfloat16)
        proj_grad = jnp.stack([query_grad_b, key_grad_b, value_grad_b], axis=1).reshape(
            -1, 3 * cols_here
        )
        pair_grad = jnp.stack(
            [
                jnp.sum(query_grad_b, axis=0, dtype=jnp.float32),
                jnp.sum(value_grad_b, axis=0, dtype=jnp.float32),
            ],
            axis=0,
        )
        qkv_grad = jnp.einsum(
            "td,tc->dc", attn_rows, proj_grad, preferred_element_type=jnp.float32
        ).reshape(model_width, 3, cols_here)
        attn_in_grad = reduce_grads(proj_grad, qkv_here, local_rows)
        attn_gain_grad = jnp.sum(attn_in_grad * attn_normal, axis=0)
        attn_bias_grad = jnp.sum(attn_in_grad, axis=0)
        gradient = middle_grad + norm_back(
            attn_in_grad, attn_normal, attn_factor, ln_attn_gain[layer_index]
        )
        sharded_list.insert(
            0,
            (
                qkv_grad,
                pair_grad,
                out_grad,
                first_grad,
                first_shift_grad,
                hidden_gain_grad,
                hidden_shift_grad,
                second_grad,
            ),
        )
        shared_list.insert(
            0,
            (
                attn_gain_grad,
                attn_bias_grad,
                scale_grad,
                out_shift_grad,
                post_gain_grad,
                post_bias_grad,
                ffn_gain_grad,
                ffn_bias_grad,
                second_shift_grad,
            ),
        )
    sharded = stack_layers(sharded_list, 8)
    shared = stack_layers(shared_list, 9)
    sharded = (
        lax.psum(sharded[0].astype(jnp.bfloat16), "rows").astype(jnp.float32),
        lax.psum(sharded[1].astype(jnp.bfloat16), "rows").astype(jnp.float32),
        lax.psum(sharded[2].astype(jnp.bfloat16), "rows").astype(jnp.float32),
        lax.psum(sharded[3].astype(jnp.bfloat16), "rows").astype(jnp.float32),
        lax.psum(sharded[4].astype(jnp.bfloat16), "rows").astype(jnp.float32),
        lax.psum(sharded[5].astype(jnp.bfloat16), "rows").astype(jnp.float32),
        lax.psum(sharded[6].astype(jnp.bfloat16), "rows").astype(jnp.float32),
        lax.psum(sharded[7].astype(jnp.bfloat16), "rows").astype(jnp.float32),
    )
    shared = lax.psum(
        (
            shared[0],
            shared[1],
            shared[2],
            shared[3],
            shared[4],
            shared[5],
            shared[6],
            shared[7],
            shared[8],
        ),
        ("rows", "mp"),
    )
    return (
        layer_output,
        gradient,
        shared[0],
        shared[1],
        sharded[0],
        sharded[1],
        shared[2],
        sharded[2],
        shared[3],
        shared[4],
        shared[5],
        shared[6],
        shared[7],
        sharded[3],
        sharded[4],
        sharded[5],
        sharded[6],
        sharded[7],
        shared[8],
    )


def solution(mesh):
    in_specs = (
        P(("rows", "mp"), None),
        P("rows"),
        P(("rows", "mp"), None),
        P(),
        P(),
        P(None, None, None, "mp"),
        P(None, None, "mp"),
        P(),
        P(None, "mp", None),
        P(),
        P(),
        P(),
        P(),
        P(),
        P(None, None, "mp"),
        P(None, "mp"),
        P(None, "mp"),
        P(None, "mp"),
        P(None, "mp", None),
        P(),
    )
    out_specs = (
        P(("rows", "mp"), None),
        P(("rows", "mp"), None),
        P(),
        P(),
        P(None, None, None, "mp"),
        P(None, None, "mp"),
        P(),
        P(None, "mp", None),
        P(),
        P(),
        P(),
        P(),
        P(),
        P(None, None, "mp"),
        P(None, "mp"),
        P(None, "mp"),
        P(None, "mp"),
        P(None, "mp", None),
        P(),
    )
    return jax.shard_map(
        per_device, mesh=mesh, in_specs=in_specs, out_specs=out_specs, check_vma=False
    )
```

profile of v0, /device:TPU:1, one launch (start us, length us, event | category | flops | bytes accessed | tf_op | source)
XLA Modules:
  0.0 2364.8 jit_solution(18262623674828010216)
XLA Ops:
  18.1 71.0 %all-gather.9.cloned.1.call-done = bf16[2048,1024]{1,0:T(8,128)(2,1)} async-done(((bf16[256,1024]{1,0:T(8,128)(2,1)}), bf16[2048,1024]{1,0:T(8,128)(2,1)}) %all-gather.9.cloned.1.call-update) | async-done | bytes 4194320 | tf_op jit(solution)/shard_map/all_gather | solution.py:32
  123.2 36.4 %while.60 = (s32[]{:T(128)}, f32[2,512,4,64]{1,3,2,0:T(8,128)}, f32[2,4,512]{2,1,0:T(4,128)S(1)}, s32[2]{0:T(128)S(1)}, s32[]{:T(128)}, /*index=5*/s32[2048]{0:T...) while((s32[]{:T(128)}, f32[2,512,4,64]{1,3,2,0:T(8,128)}, ...), condition=%wide.region_5.6_spmd.clone, body=%wide.region_2.5_spmd.clone.sunk | while | flops 1127217664 | bytes 65882412 | solution.py:128
  176.1 88.5 %reduce-scatter.9.cloned.1.call-done = bf16[256,1024]{1,0:T(8,128)(2,1)} async-done(((bf16[2048,1024]{1,0:T(8,128)(2,1)}), bf16[256,1024]{1,0:T(8,128)(2,1)}) %reduce-scatter.9.cloned.1.call-update) | async-done | bytes 524304 | tf_op jit(solution)/shard_map/reduce_scatter | solution.py:44
  274.9 70.2 %all-gather.11.cloned.1.call-done = bf16[2048,1024]{1,0:T(8,128)(2,1)} async-done(((bf16[256,1024]{1,0:T(8,128)(2,1)}), bf16[2048,1024]{1,0:T(8,128)(2,1)}) %all-gather.11.cloned.1.call-update) | async-done | bytes 4194320 | tf_op jit(solution)/shard_map/all_gather | solution.py:32
  361.2 28.4 %all-reduce.4 = (f32[2048]{0:T(1024)S(1)}, f32[2048]{0:T(1024)S(1)}) all-reduce(f32[2048]{0:T(1024)S(1)} %get-tuple-element.594, f32[2048]{0:T(1024)S(1)} %get-tuple-element.593), channel_id=1, replica_groups=mesh['rows'=4,'mp'=8] {'mp'}, use_global_device_ids=true, to_apply=%region_15.16 | all-reduce | flops 4096 | bytes 32768 | tf_op jit(solution)/shard_map/psum | solution.py:66
  398.1 91.5 %reduce-scatter.11.cloned.1.call-done = bf16[256,1024]{1,0:T(8,128)(2,1)} async-done(((bf16[2048,1024]{1,0:T(8,128)(2,1)}), bf16[256,1024]{1,0:T(8,128)(2,1)}) %reduce-scatter.11.cloned.1.call-update) | async-done | bytes 524304 | tf_op jit(solution)/shard_map/reduce_scatter | solution.py:44
  493.8 71.7 %all-gather.13.cloned.1.call-done = bf16[2048,1024]{1,0:T(8,128)(2,1)} async-done(((bf16[256,1024]{1,0:T(8,128)(2,1)}), bf16[2048,1024]{1,0:T(8,128)(2,1)}) %all-gather.13.cloned.1.call-update) | async-done | bytes 4194320 | tf_op jit(solution)/shard_map/all_gather | solution.py:32
  600.2 36.6 %while.61 = (s32[]{:T(128)}, f32[2,512,4,64]{1,3,2,0:T(8,128)}, f32[2,4,512]{2,1,0:T(4,128)}, s32[2]{0:T(128)S(1)}, s32[]{:T(128)}, /*index=5*/s32[2048]{0:T(102...) while((s32[]{:T(128)}, f32[2,512,4,64]{1,3,2,0:T(8,128)}, ...), condition=%wide.region_22.23_spmd.clone, body=%wide.region_19.22_spmd.clone.sunk | while | flops 1127217664 | bytes 65882412 | solution.py:128
  649.5 91.1 %reduce-scatter.13.cloned.1.call-done = bf16[256,1024]{1,0:T(8,128)(2,1)} async-done(((bf16[2048,1024]{1,0:T(8,128)(2,1)}), bf16[256,1024]{1,0:T(8,128)(2,1)}) %reduce-scatter.13.cloned.1.call-update) | async-done | bytes 524304 | tf_op jit(solution)/shard_map/reduce_scatter | solution.py:44
  747.3 67.7 %all-gather.17.cloned.1.call-done = bf16[2048,1024]{1,0:T(8,128)(2,1)} async-done(((bf16[256,1024]{1,0:T(8,128)(2,1)}), bf16[2048,1024]{1,0:T(8,128)(2,1)}) %all-gather.17.cloned.1.call-update) | async-done | bytes 4194320 | tf_op jit(solution)/shard_map/all_gather | solution.py:36
  827.8 61.7 %all-gather.15.cloned.1.call-done = bf16[2048,1024]{1,0:T(8,128)(2,1)} async-done(((bf16[256,1024]{1,0:T(8,128)(2,1)}), bf16[2048,1024]{1,0:T(8,128)(2,1)}) %all-gather.15.cloned.1.call-update) | async-done | bytes 4194320 | tf_op jit(solution)/shard_map/all_gather | solution.py:32
  988.2 91.5 %reduce-scatter.17.cloned.1.call-done = bf16[256,1024]{1,0:T(8,128)(2,1)} async-done(((bf16[2048,1024]{1,0:T(8,128)(2,1)}), bf16[256,1024]{1,0:T(8,128)(2,1)}) %reduce-scatter.17.cloned.1.call-update) | async-done | bytes 524304 | tf_op jit(solution)/shard_map/reduce_scatter | solution.py:57
  1082.2 88.6 %reduce-scatter.15.cloned.1.call-done = bf16[256,1024]{1,0:T(8,128)(2,1)} async-done(((bf16[2048,1024]{1,0:T(8,128)(2,1)}), bf16[256,1024]{1,0:T(8,128)(2,1)}) %reduce-scatter.15.cloned.1.call-update) | async-done | bytes 524304 | tf_op jit(solution)/shard_map/reduce_scatter | solution.py:44
  1177.0 72.0 %all-gather.19.cloned.1.call-done = bf16[2048,1024]{1,0:T(8,128)(2,1)} async-done(((bf16[256,1024]{1,0:T(8,128)(2,1)}), bf16[2048,1024]{1,0:T(8,128)(2,1)}) %all-gather.19.cloned.1.call-update) | async-done | bytes 4194320 | tf_op jit(solution)/shard_map/all_gather | solution.py:36
  1264.1 130.2 %while.62 = (s32[]{:T(128)}, f32[2048,4,64]{0,2,1:T(8,128)}, f32[2048,4,64]{0,2,1:T(8,128)}, bf16[2,512,4,64]{1,0,3,2:T(2,128)(2,1)}, s32[2]{0:T(128)S(1)}, /*in...) while((s32[]{:T(128)}, f32[2048,4,64]{0,2,1:T(8,128)}, ...), condition=%wide.region_45.46_spmd.clone, body=%wide.region_43.45_spmd.clone.sunk | while | flops 2753296896 | bytes 236268144 | solution.py:175
  1428.7 92.3 %reduce-scatter.19.cloned.1.call-done = bf16[256,1024]{1,0:T(8,128)(2,1)} async-done(((bf16[2048,1024]{1,0:T(8,128)(2,1)}), bf16[256,1024]{1,0:T(8,128)(2,1)}) %reduce-scatter.19.cloned.1.call-update) | async-done | bytes 524304 | tf_op jit(solution)/shard_map/reduce_scatter | solution.py:57
  1526.2 72.0 %all-gather.21.cloned.1.call-done = bf16[2048,1024]{1,0:T(8,128)(2,1)} async-done(((bf16[256,1024]{1,0:T(8,128)(2,1)}), bf16[2048,1024]{1,0:T(8,128)(2,1)}) %all-gather.21.cloned.1.call-update) | async-done | bytes 4194320 | tf_op jit(solution)/shard_map/all_gather | solution.py:36
  1616.5 28.4 %all-reduce.1 = (f32[2048]{0:T(1024)S(1)}, f32[2048]{0:T(1024)S(1)}) all-reduce(f32[2048]{0:T(1024)S(1)} %get-tuple-element.586, f32[2048]{0:T(1024)S(1)} %get-tuple-element.590), channel_id=1, replica_groups=mesh['rows'=4,'mp'=8] {'mp'}, use_global_device_ids=true, to_apply=%region_52.53 | all-reduce | flops 4096 | bytes 32768 | tf_op jit(solution)/shard_map/psum | solution.py:70
  1659.4 92.6 %reduce-scatter.21.cloned.1.call-done = bf16[256,1024]{1,0:T(8,128)(2,1)} async-done(((bf16[2048,1024]{1,0:T(8,128)(2,1)}), bf16[256,1024]{1,0:T(8,128)(2,1)}) %reduce-scatter.21.cloned.1.call-update) | async-done | bytes 524304 | tf_op jit(solution)/shard_map/reduce_scatter | solution.py:57
  1781.9 49.4 %all-gather.23.cloned.1.call-done = bf16[2048,1024]{1,0:T(8,128)(2,1)} async-done(((bf16[256,1024]{1,0:T(8,128)(2,1)}), bf16[2048,1024]{1,0:T(8,128)(2,1)}) %all-gather.23.cloned.1.call-update) | async-done | bytes 4194320 | tf_op jit(solution)/shard_map/all_gather | solution.py:36
  1843.8 121.0 %while.63 = (s32[]{:T(128)}, f32[2048,4,64]{0,2,1:T(8,128)}, f32[2048,4,64]{0,2,1:T(8,128)}, bf16[2,512,4,64]{1,0,3,2:T(2,128)(2,1)}, s32[2]{0:T(128)S(1)}, /*in...) while((s32[]{:T(128)}, f32[2048,4,64]{0,2,1:T(8,128)}, ...), condition=%wide.region_60.61_spmd.clone, body=%wide.region_58.60_spmd.clone.sunk | while | flops 2753296896 | bytes 232073840 | solution.py:175
  2026.3 95.7 %all-reduce.12.cloned.1.call-done = (bf16[2,1024,3,128]{3,1,2,0:T(8,128)(2,1)}, bf16[2,128,1024]{2,1,0:T(8,128)(2,1)}, bf16[2,1024,512]{2,1,0:T(8,128)(2,1)}, bf16[2,512,1024]{2,1,0:T(8,128)(2,1)}) async-done(((bf16[2,1024,3,128]{3,1,2,0:T(8,128)(2,1)}, bf16[2,128,1024]{2,1,0:T(8,128)(2,1)}, bf16[2,1024,512]{2,1,0:T(8,128)(2,1)}, bf16[2,512,1024]{2,1,0:T(8,128)(2,1)}), (bf16[2,1024,3,128]{3,1,2,0:T(8,128)(2,1)}, ...) | async-done | bytes 6291472 | tf_op jit(solution)/shard_map/psum | solution.py:463
  2132.7 81.8 %reduce-scatter.23.cloned.1.call-done = bf16[256,1024]{1,0:T(8,128)(2,1)} async-done(((bf16[2048,1024]{1,0:T(8,128)(2,1)}), bf16[256,1024]{1,0:T(8,128)(2,1)}) %reduce-scatter.23.cloned.1.call-update) | async-done | bytes 524304 | tf_op jit(solution)/shard_map/reduce_scatter | solution.py:57
  2219.7 126.5 %all-reduce.10.cloned.1.call-done = (f32[2,1024]{1,0:T(2,128)}, f32[2,1024]{1,0:T(2,128)}, f32[2,16]{1,0:T(2,128)}, f32[2,1024]{1,0:T(2,128)}, f32[2,1024]{1,0:T...) async-done(((f32[2,1024]{1,0:T(2,128)}, f32[2,1024]{1,0:T(2,128)}, f32[2,16]{1,0:T(2,128)}, f32[2,1024]{1,0:T(2,128)}, ...) | async-done | bytes 65680 | tf_op jit(solution)/shard_map/psum | solution.py:472
  (767 shorter events, 783.7 us)
Async XLA Ops:
  7.2 81.9 %all-gather.9.cloned.1.call-start = ((), (), s32[]{:S(2)}) async-start(), calls=%async_computation.8 | async-start | bytes 4718592 | tf_op jit(solution)/shard_map/all_gather | solution.py:32
  14.7 249.9 %reduce-scatter.9.cloned.1.call-start = ((), (), s32[]{:S(2)}) async-start(), calls=%async_computation.9 | async-start | bytes 4718592 | tf_op jit(solution)/shard_map/reduce_scatter | solution.py:44
  94.9 15.8 collective-permute-start.1
  96.7 25.2 %collective-permute-start.2 = (bf16[2048,128]{0,1:T(8,128)(2,1)S(1)}, bf16[2048,128]{0,1:T(8,128)(2,1)S(1)}, u32[]{:S(2)}, u32[]{:S(2)}) collective-permute-start(bf16[2048,128]{0,1:T(8,128)(2,1)S(1)} %get-tuple-element.774), channel_id=1, source_target_pairs={{0,1},{1,0},{2,3},{3,2},{4,5},{5,4},{6,7},{7,6},{8,9},{9,8},{10,11... | collective-permute-start | bytes 1572872 | tf_op jit(solution)/shard_map/ppermute | solution.py:13
  172.5 172.6 %all-gather.11.cloned.1.call-start = ((), (), s32[]{:S(2)}) async-start(), calls=%async_computation.10 | async-start | bytes 4718592 | tf_op jit(solution)/shard_map/all_gather | solution.py:32
  273.0 216.6 %reduce-scatter.11.cloned.1.call-start = ((), (), s32[]{:S(2)}) async-start(), calls=%async_computation.11 | async-start | bytes 4718592 | tf_op jit(solution)/shard_map/reduce_scatter | solution.py:44
  396.9 168.5 %all-gather.13.cloned.1.call-start = ((), (), s32[]{:S(2)}) async-start(), calls=%async_computation.12 | async-start | bytes 4718592 | tf_op jit(solution)/shard_map/all_gather | solution.py:32
  493.4 247.3 %reduce-scatter.13.cloned.1.call-start = ((), (), s32[]{:S(2)}) async-start(), calls=%async_computation.13 | async-start | bytes 4718592 | tf_op jit(solution)/shard_map/reduce_scatter | solution.py:44
  571.2 15.9 collective-permute-start.5
  572.3 25.9 %collective-permute-start.6 = (bf16[2048,128]{0,1:T(8,128)(2,1)S(1)}, bf16[2048,128]{0,1:T(8,128)(2,1)S(1)}, u32[]{:S(2)}, u32[]{:S(2)}) collective-permute-start(bf16[2048,128]{0,1:T(8,128)(2,1)S(1)} %get-tuple-element.772), channel_id=1, source_target_pairs={{0,1},{1,0},{2,3},{3,2},{4,5},{5,4},{6,7},{7,6},{8,9},{9,8},{10,11... | collective-permute-start | bytes 1572872 | tf_op jit(solution)/shard_map/ppermute | solution.py:13
  648.7 166.2 %all-gather.17.cloned.1.call-start = ((), (), s32[]{:S(2)}) async-start(), calls=%async_computation.16 | async-start | bytes 4718592 | tf_op jit(solution)/shard_map/all_gather | solution.py:36
  649.5 240.1 %all-gather.15.cloned.1.call-start = ((), (), s32[]{:S(2)}) async-start(), calls=%async_computation.14 | async-start | bytes 4718592 | tf_op jit(solution)/shard_map/all_gather | solution.py:32
  747.1 332.6 %reduce-scatter.17.cloned.1.call-start = ((), (), s32[]{:S(2)}) async-start(), calls=%async_computation.17 | async-start | bytes 4718592 | tf_op jit(solution)/shard_map/reduce_scatter | solution.py:57
  980.3 190.6 %reduce-scatter.15.cloned.1.call-start = ((), (), s32[]{:S(2)}) async-start(), calls=%async_computation.15 | async-start | bytes 4718592 | tf_op jit(solution)/shard_map/reduce_scatter | solution.py:44
  988.1 260.9 %all-gather.19.cloned.1.call-start = ((), (), s32[]{:S(2)}) async-start(), calls=%async_computation.18 | async-start | bytes 4718592 | tf_op jit(solution)/shard_map/all_gather | solution.py:36
  1176.9 344.0 %reduce-scatter.19.cloned.1.call-start = ((), (), s32[]{:S(2)}) async-start(), calls=%async_computation.19 | async-start | bytes 4718592 | tf_op jit(solution)/shard_map/reduce_scatter | solution.py:57
  1400.5 22.7 collective-permute-start.10
  1428.6 169.6 %all-gather.21.cloned.1.call-start = ((), (), s32[]{:S(2)}) async-start(), calls=%async_computation.20 | async-start | bytes 4718592 | tf_op jit(solution)/shard_map/all_gather | solution.py:36
  1526.1 226.0 %reduce-scatter.21.cloned.1.call-start = ((), (), s32[]{:S(2)}) async-start(), calls=%async_computation.21 | async-start | bytes 4718592 | tf_op jit(solution)/shard_map/reduce_scatter | solution.py:57
  1659.4 171.9 %all-gather.23.cloned.1.call-start = ((), (), s32[]{:S(2)}) async-start(), calls=%async_computation.22 | async-start | bytes 4718592 | tf_op jit(solution)/shard_map/all_gather | solution.py:36
  1759.3 362.7 %all-reduce.12.cloned.1.call-start = ((), (), s32[]{:S(2)}) async-start(), calls=%async_computation.25 | async-start | bytes 12582912 | tf_op jit(solution)/shard_map/psum | solution.py:463
  1971.0 22.7 collective-permute-start.14
  1997.5 216.9 %reduce-scatter.23.cloned.1.call-start = ((), (), s32[]{:S(2)}) async-start(), calls=%async_computation.23 | async-start | bytes 4718592 | tf_op jit(solution)/shard_map/reduce_scatter | solution.py:57
  2003.3 342.9 %all-reduce.10.cloned.1.call-start = ((), (), s32[]{:S(2)}) async-start(), calls=%async_computation.24 | async-start | bytes 133120 | tf_op jit(solution)/shard_map/psum | solution.py:472
  (207 other events, 7478.3 us)
Sparse Core Ops, SparseCore 0:
  14.8 74.2 all-gather.8
  172.6 91.9 reduce-scatter.8
  273.1 71.8 all-gather.10
  397.0 92.5 reduce-scatter.10
  493.5 71.8 all-gather.12
  648.8 91.7 reduce-scatter.12
  743.0 71.8 all-gather.16
  817.9 71.6 all-gather.14
  980.4 99.2 reduce-scatter.16
  1083.2 87.6 reduce-scatter.14
  1177.1 71.9 all-gather.18
  1428.7 92.1 reduce-scatter.18
  1526.2 71.9 all-gather.20
  1659.5 92.5 reduce-scatter.20
  1759.4 71.8 all-gather.22
  1997.7 124.2 all-reduce.11
  2125.9 88.5 reduce-scatter.22
  2222.4 123.7 all-reduce.9
where the time goes:
time: 2370 us; the launch traced here: 2360 us
  waiting for transfers between devices  1580 us (67%)
  matrix products  265 us (11%)
  other arithmetic  195 us (8%)
  local copies, waits for them, and re-layouts  141 us (6%)
  blocking collectives  121 us (5%)
  loops' own time  31.7 us (1%)
    reduce_scatter x4, waiting for transfers between devices, reduce_branch(): lax.psum_scatter(partial_term(jnp.int32(0), local_rows * lax.axis_size('m...  360 us
    reduce_scatter x4, waiting for transfers between devices, reduce_grads(): lax.psum_scatter(partial_term(jnp.int32(0), local_rows * lax.axis_size('m...  358 us
    all_gather x4, waiting for transfers between devices, collect_rows(): return lax.all_gather(normed_b, 'mp', axis=0, tiled=True)  275 us
    all_gather x4, waiting for transfers between devices, collect_grads(): return lax.all_gather(gradient_b, 'mp', axis=0, tiled=True)  261 us
    psum x1, waiting for transfers between devices, per_device(): lax.psum((shared[0], shared[1], shared[2], shared[3], shared[4], shared[5...  126 us
    ppermute x16, waiting for transfers between devices, partner(): lax.ppermute(shard, axis, [(i, i ^ 1 << stride) for i in range(lax.axis_s...  107 us
    psum x1, waiting for transfers between devices, per_device(): lax.psum(sharded[0].astype(jnp.bfloat16), 'rows').astype(jnp.float32)  95.7 us
    psum x2, blocking collectives, hidden_stats(): return lax.psum((first_sum, second_sum), 'mp')  56.9 us
  transfers between devices with their start and end apart: 34, of which 32 were waited for; matrix products, arithmetic and copies ran while one was open for 4% of the time, Pallas kernels for 0%

commit v1 on v0

--- a/solution.py
+++ b/solution.py
@@ -3,6 +3,9 @@
 import jax
 import jax.numpy as jnp
 from jax import lax
+from jax.experimental import pallas as pl
+from jax.experimental.pallas import tpu as pltpu
+from jax.sharding import Mesh
 from jax.sharding import PartitionSpec as P
 
 epsilon = 1e-05
@@ -506,50 +509,877 @@
     )
 
 
+MESH_ID = pl.DeviceIdType.MESH
+PLANE = ("core", "y", "x")
+EVERY = ("y", "core", "z", "x")
+f32 = jnp.float32
+bf16 = jnp.bfloat16
+
+
+def vmem_params(collective_id=None, mib=48):
+    if collective_id is None:
+        return pltpu.CompilerParams(vmem_limit_bytes=mib * 2**20)
+    return pltpu.CompilerParams(
+        vmem_limit_bytes=mib * 2**20, collective_id=collective_id, has_side_effects=True
+    )
+
+
+def plane_pairs():
+    pairs = []
+    for y in range(2):
+        for core in range(2):
+            for z in range(4):
+                for x in range(2):
+                    source = ((y * 2 + core) * 4 + z) * 2 + x
+                    target = (((z % 2) * 2 + z // 2) * 4 + (2 * y + core)) * 2 + x
+                    pairs.append((source, target))
+    return pairs
+
+
+def to_plane(values):
+    return lax.ppermute(values, EVERY, plane_pairs())
+
+
+def from_plane(values):
+    return lax.ppermute(values, EVERY, [(target, source) for source, target in plane_pairs()])
+
+
+def greet(peers):
+    barrier = pltpu.get_barrier_semaphore()
+    for peer in peers:
+        pl.semaphore_signal(barrier, inc=1, device_id=peer, device_id_type=MESH_ID)
+    pl.semaphore_wait(barrier, len(peers))
+
+
+def gather_kernel(x_ref, o_ref, send_sem, recv_sem, own_sem):
+    rows = x_ref.shape[0]
+    half = rows // 2
+    x, y, core = lax.axis_index("x"), lax.axis_index("y"), lax.axis_index("core")
+    to_x, to_y, to_core = {"x": 1 - x}, {"y": 1 - y}, {"core": 1 - core}
+    greet((to_x, to_y, to_core))
+
+    def place(at_x, at_y, part=None):
+        first = ((2 * core + at_y) * 2 + at_x) * rows
+        if part is None:
+            return o_ref.at[pl.ds(pl.multiple_of(first, rows), rows)]
+        return o_ref.at[pl.ds(pl.multiple_of(first + part * half, half), half)]
+
+    def copy(index, source, target, peer):
+        return pltpu.make_async_remote_copy(
+            src_ref=source,
+            dst_ref=target,
+            send_sem=send_sem.at[index],
+            recv_sem=recv_sem.at[index],
+            device_id=peer,
+            device_id_type=MESH_ID,
+        )
+
+    own = place(x, y)
+    copy_0 = copy(0, x_ref, own, to_x)
+    copy_1 = copy(1, x_ref, own, to_y)
+    copy_2 = copy(2, x_ref, own, to_core)
+    copy_0.start()
+    copy_1.start()
+    copy_2.start()
+    keep = pltpu.make_async_copy(x_ref, own, own_sem)
+    keep.start()
+    copy_0.wait_recv()
+    copy_4 = copy(4, place(1 - x, y, 0), place(1 - x, y, 0), to_y)
+    copy_3 = copy(3, place(1 - x, y), place(1 - x, y), to_core)
+    copy_4.start()
+    copy_3.start()
+    copy_1.wait_recv()
+    copy_6 = copy(6, place(x, 1 - y, 1), place(x, 1 - y, 1), to_x)
+    copy_5 = copy(5, place(x, 1 - y), place(x, 1 - y), to_core)
+    copy_6.start()
+    copy_5.start()
+    copy_4.wait_recv()
+    copy_7 = copy(7, place(1 - x, 1 - y, 0), place(1 - x, 1 - y, 0), to_core)
+    copy_7.start()
+    copy_6.wait_recv()
+    copy_8 = copy(8, place(1 - x, 1 - y, 1), place(1 - x, 1 - y, 1), to_core)
+    copy_8.start()
+    for arriving in (copy_2, copy_3, copy_5, copy_7, copy_8):
+        arriving.wait_recv()
+    for sent in (copy_0, copy_1, copy_2, copy_3, copy_4, copy_5, copy_6, copy_7, copy_8):
+        sent.wait_send()
+    keep.wait()
+
+
+def plane_gather(block_b):
+    rows, width = block_b.shape
+    return pl.pallas_call(
+        gather_kernel,
+        out_shape=jax.ShapeDtypeStruct((8 * rows, width), block_b.dtype),
+        in_specs=[pl.BlockSpec(memory_space=pltpu.VMEM)],
+        out_specs=pl.BlockSpec(memory_space=pltpu.VMEM),
+        scratch_shapes=[
+            pltpu.SemaphoreType.DMA((9,)),
+            pltpu.SemaphoreType.DMA((9,)),
+            pltpu.SemaphoreType.DMA,
+        ],
+        compiler_params=vmem_params(1),
+    )(block_b)
+
+
+def scatter_kernel(
+    weight_dim,
+    a_ref,
+    w_ref,
+    o_ref,
+    sib_out,
+    sib_in,
+    diag_out,
+    diag_in,
+    last_x_out,
+    last_y_out,
+    last_x_in,
+    last_y_in,
+    wait_x,
+    wait_y,
+    send_sem,
+    recv_sem,
+):
+    rows = o_ref.shape[0]
+    half = rows // 2
+    x, y, core = lax.axis_index("x"), lax.axis_index("y"), lax.axis_index("core")
+    to_x, to_y, to_core = {"x": 1 - x}, {"y": 1 - y}, {"core": 1 - core}
+    greet((to_x, to_y, to_core))
+
+    def term(at_core, at_x, at_y):
+        first = pl.multiple_of(((2 * at_core + at_y) * 2 + at_x) * rows, rows)
+        return lax.dot_general(
+            a_ref[pl.ds(first, rows), :],
+            w_ref[...],
+            (((1,), (weight_dim,)), ((), ())),
+            preferred_element_type=f32,
+        )
+
+    def copy(index, source, target, peer):
+        return pltpu.make_async_remote_copy(
+            src_ref=source,
+            dst_ref=target,
+            send_sem=send_sem.at[index],
+            recv_sem=recv_sem.at[index],
+            device_id=peer,
+            device_id_type=MESH_ID,
+        )
+
+    places = ((1 - x, 1 - y), (1 - x, y), (x, 1 - y), (x, y))
+    siblings = [copy(i, sib_out.at[i], sib_in.at[i], to_core) for i in range(4)]
+
+    def help_sibling(i):
+        sib_out[i] = term(1 - core, *places[i]).astype(bf16)
+        siblings[i].start()
+
+    def joined(i):
+        mine = term(core, *places[i])
+        siblings[i].wait_recv()
+        return mine + sib_in[i].astype(f32)
+
+    help_sibling(0)
+    help_sibling(1)
+    total = joined(0)
+    diag_out[...] = total.astype(bf16)
+    diag_x = copy(4, diag_out.at[pl.ds(0, half)], diag_in.at[0], to_x)
+    diag_y = copy(5, diag_out.at[pl.ds(half, half)], diag_in.at[1], to_y)
+    diag_x.start()
+    diag_y.start()
+    help_sibling(2)
+    total = joined(1)
+    last_x_out[0] = total[:half].astype(bf16)
+    x_0 = copy(6, last_x_out.at[0], last_x_in.at[0], to_x)
+    x_0.start()
+    wait_x[...] = total[half:]
+    help_sibling(3)
+    total = joined(2)
+    last_y_out[1] = total[half:].astype(bf16)
+    y_1 = copy(7, last_y_out.at[1], last_y_in.at[1], to_y)
+    y_1.start()
+    wait_y[...] = total[:half]
+    diag_y.wait_recv()
+    last_x_out[1] = (wait_x[...] + diag_in[1].astype(f32)).astype(bf16)
+    x_1 = copy(8, last_x_out.at[1], last_x_in.at[1], to_x)
+    x_1.start()
+    diag_x.wait_recv()
+    last_y_out[0] = (wait_y[...] + diag_in[0].astype(f32)).astype(bf16)
+    y_0 = copy(9, last_y_out.at[0], last_y_in.at[0], to_y)
+    y_0.start()
+    o_ref[...] = joined(3)
+    x_0.wait_recv()
+    y_1.wait_recv()
+    x_1.wait_recv()
+    y_0.wait_recv()
+    for part in range(2):
+        piece = pl.ds(part * half, half)
+        o_ref[piece, :] += last_x_in[part].astype(f32) + last_y_in[part].astype(f32)
+    for sent in (*siblings, diag_x, diag_y, x_0, y_1, x_1, y_0):
+        sent.wait_send()
+
+
+def plane_scatter(operand_b, weight_b, weight_dim, collective_id):
+    rows = operand_b.shape[0] // 8
+    half = rows // 2
+    width = weight_b.shape[1 - weight_dim]
+    return pl.pallas_call(
+        partial(scatter_kernel, weight_dim),
+        out_shape=jax.ShapeDtypeStruct((rows, width), f32),
+        in_specs=[pl.BlockSpec(memory_space=pltpu.VMEM)] * 2,
+        out_specs=pl.BlockSpec(memory_space=pltpu.VMEM),
+        scratch_shapes=[
+            pltpu.VMEM((4, rows, width), bf16),
+            pltpu.VMEM((4, rows, width), bf16),
+            pltpu.VMEM((rows, width), bf16),
+            pltpu.VMEM((2, half, width), bf16),
+            pltpu.VMEM((2, half, width), bf16),
+            pltpu.VMEM((2, half, width), bf16),
+            pltpu.VMEM((2, half, width), bf16),
+            pltpu.VMEM((2, half, width), bf16),
+            pltpu.VMEM((half, width), f32),
+            pltpu.VMEM((half, width), f32),
+            pltpu.SemaphoreType.DMA((10,)),
+            pltpu.SemaphoreType.DMA((10,)),
+        ],
+        compiler_params=vmem_params(collective_id),
+    )(operand_b, weight_b)
+
+
+def plane_sum_kernel(v_ref, o_ref, got, send_sem, recv_sem):
+    x, y, core = lax.axis_index("x"), lax.axis_index("y"), lax.axis_index("core")
+    peers = []
+    for flip in range(1, 8):
+        at_x = 1 - x if flip & 1 else x
+        at_y = 1 - y if flip & 2 else y
+        at_core = 1 - core if flip & 4 else core
+        peers.append({"x": at_x, "y": at_y, "core": at_core})
+    greet(peers)
+    me = (2 * core + y) * 2 + x
+    copies = []
+    for index, peer in enumerate(peers):
+        copies.append(
+            pltpu.make_async_remote_copy(
+                src_ref=v_ref,
+                dst_ref=got.at[index],
+                send_sem=send_sem.at[index],
+                recv_sem=recv_sem.at[index],
+                device_id=peer,
+                device_id_type=MESH_ID,
+            )
+        )
+    for each in copies:
+        each.start()
+    for each in copies:
+        each.wait_recv()
+    by_x = [v_ref[...] + got[0]]
+    for flip in (2, 4, 6):
+        by_x.append(got[flip - 1] + got[flip])
+    o_ref[...] = (by_x[0] + by_x[1]) + (by_x[2] + by_x[3])
+    for each in copies:
+        each.wait_send()
+
+
+def plane_sum(values):
+    return pl.pallas_call(
+        plane_sum_kernel,
+        out_shape=jax.ShapeDtypeStruct(values.shape, f32),
+        in_specs=[pl.BlockSpec(memory_space=pltpu.VMEM)],
+        out_specs=pl.BlockSpec(memory_space=pltpu.VMEM),
+        scratch_shapes=[
+            pltpu.VMEM((7, *values.shape), f32),
+            pltpu.SemaphoreType.DMA((7,)),
+            pltpu.SemaphoreType.DMA((7,)),
+        ],
+        compiler_params=vmem_params(6),
+    )(values)
+
+
+BLOCK = 256
+
+
+def head_masks(head_width, width):
+    lane = lax.broadcasted_iota(jnp.int32, (1, width), 1)
+    lower = (lane < head_width).astype(bf16)
+    return lower, (1 - lower).astype(bf16)
+
+
+def attend_kernel(head_width, q_ref, k_ref, v_ref, dq_ref, dk_ref, o_ref, l_ref, s_buf, acc, top):
+    block = pl.program_id(0)
+    width = q_ref.shape[1]
+    low_mask, high_mask = head_masks(head_width, width)
+    q = q_ref[...]
+    pair = jnp.concatenate([q * low_mask, q * high_mask], axis=0)
+    top[...] = jnp.full_like(top, masked)
+
+    def scores(at):
+        keys = k_ref[pl.ds(pl.multiple_of(at * BLOCK, BLOCK), BLOCK), :]
+        return lax.dot_general(pair, keys, (((1,), (1,)), ((), ())), preferred_element_type=f32)
+
+    def first_pass(at, carry):
+        s = scores(at)
+        s_buf[at] = s
+        top[...] = jnp.maximum(top[...], jnp.maximum(s[:, :128], s[:, 128:]))
+        return carry
+
+    lax.fori_loop(0, block, first_pass, 0)
+    docs = dq_ref[...]
+    docs = jnp.concatenate([docs, docs], axis=0)
+    place = lax.broadcasted_iota(jnp.int32, (2 * BLOCK, BLOCK), 0)
+    place = jnp.where(place >= BLOCK, place - BLOCK, place)
+    allowed = (docs == dk_ref[...]) & (
+        place >= lax.broadcasted_iota(jnp.int32, (2 * BLOCK, BLOCK), 1)
+    )
+    s = jnp.where(allowed, scores(block), masked)
+    shift = jnp.where(docs == 0, 0.0, masked)
+    peak = jnp.maximum(
+        jnp.max(top[...], axis=1, keepdims=True) + shift, jnp.max(s, axis=1, keepdims=True)
+    )
+    p = jnp.exp(s - peak)
+    top[...] = p[:, :128] + p[:, 128:]
+    values = v_ref[pl.ds(pl.multiple_of(block * BLOCK, BLOCK), BLOCK), :]
+    acc[...] = jnp.dot(p.astype(bf16), values, preferred_element_type=f32)
+    base = peak - shift
+
+    def second_pass(at, carry):
+        p = jnp.exp(s_buf[at] - base)
+        top[...] += p[:, :128] + p[:, 128:]
+        values = v_ref[pl.ds(pl.multiple_of(at * BLOCK, BLOCK), BLOCK), :]
+        acc[...] += jnp.dot(p.astype(bf16), values, preferred_element_type=f32)
+        return carry
+
+    lax.fori_loop(0, block, second_pass, 0)
+    total = jnp.sum(top[...], axis=1, keepdims=True)
+    out = acc[...] / total
+    lane = lax.broadcasted_iota(jnp.int32, (BLOCK, width), 1)
+    o_ref[...] = jnp.where(lane < head_width, out[:BLOCK], out[BLOCK:])
+    logs = jnp.broadcast_to(peak + jnp.log(total), (2 * BLOCK, 128))
+    l_ref[0] = jnp.transpose(logs)[0:1, :]
+
+
+def attend_plane(q, k, v, doc_col, doc_row, head_width):
+    rows, width = q.shape
+    blocks = rows // BLOCK
+    whole = pl.BlockSpec((rows, width), lambda i: (0, 0))
+    part = pl.BlockSpec((BLOCK, width), lambda i: (i, 0))
+    return pl.pallas_call(
+        partial(attend_kernel, head_width),
+        grid=(blocks,),
+        out_shape=(
+            jax.ShapeDtypeStruct((rows, width), f32),
+            jax.ShapeDtypeStruct((blocks, 1, 2 * BLOCK), f32),
+        ),
+        in_specs=[
+            part,
+            whole,
+            whole,
+            pl.BlockSpec((BLOCK, 1), lambda i: (i, 0)),
+            pl.BlockSpec((1, BLOCK), lambda i: (0, i)),
+        ],
+        out_specs=(part, pl.BlockSpec((1, 1, 2 * BLOCK), lambda i: (i, 0, 0))),
+        scratch_shapes=[
+            pltpu.VMEM((blocks, 2 * BLOCK, BLOCK), f32),
+            pltpu.VMEM((2 * BLOCK, width), f32),
+            pltpu.VMEM((2 * BLOCK, 128), f32),
+        ],
+        compiler_params=vmem_params(),
+    )(q, k, v, doc_col, doc_row)
+
+
+def attend_back_kernel(
+    head_width,
+    q_ref,
+    k_ref,
+    v_ref,
+    do_ref,
+    o_ref,
+    l_ref,
+    dcol_ref,
+    drow_ref,
+    gq_ref,
+    gk_ref,
+    gv_ref,
+    acc_k,
+    acc_v,
+    acc_q,
+):
+    block = pl.program_id(0)
+    width = q_ref.shape[1]
+    low_mask, high_mask = head_masks(head_width, width)
+    q = q_ref[...]
+    pair_q = jnp.concatenate([q * low_mask, q * high_mask], axis=0)
+    do = do_ref[...]
+    pair_do = jnp.concatenate([do * low_mask, do * high_mask], axis=0)
+    o = o_ref[...]
+    inner = jnp.sum(
+        jnp.concatenate([o, o], axis=0) * pair_do.astype(f32), axis=1, keepdims=True
+    )
+    inner = jnp.transpose(jnp.broadcast_to(inner, (2 * BLOCK, 128)))[0:1, :]
+    logs = l_ref[0]
+    docs = drow_ref[...]
+    docs = jnp.concatenate([docs, docs], axis=1)
+
+    @pl.when(block == 0)
+    def _():
+        acc_k[...] = jnp.zeros_like(acc_k)
+        acc_v[...] = jnp.zeros_like(acc_v)
+
+    def step(at, base, allowed):
+        piece = pl.ds(pl.multiple_of(at * BLOCK, BLOCK), BLOCK)
+        keys = k_ref[piece, :]
+        s = lax.dot_general(keys, pair_q, (((1,), (1,)), ((), ())), preferred_element_type=f32)
+        p = jnp.exp(s - base)
+        if allowed is not None:
+            p = jnp.where(allowed, p, 0.0)
+        dp = lax.dot_general(
+            v_ref[piece, :], pair_do, (((1,), (1,)), ((), ())), preferred_element_type=f32
+        )
+        ds = (p * (dp - inner)).astype(bf16)
+        acc_v[piece, :] += jnp.dot(p.astype(bf16), pair_do, preferred_element_type=f32)
+        acc_k[piece, :] += jnp.dot(ds, pair_q, preferred_element_type=f32)
+        return lax.dot_general(ds, keys, (((0,), (0,)), ((), ())), preferred_element_type=f32)
+
+    place = lax.broadcasted_iota(jnp.int32, (BLOCK, 2 * BLOCK), 1)
+    place = jnp.where(place >= BLOCK, place - BLOCK, place)
+    allowed = (docs == dcol_ref[...]) & (
+        place >= lax.broadcasted_iota(jnp.int32, (BLOCK, 2 * BLOCK), 0)
+    )
+    acc_q[...] = step(block, logs, allowed)
+    base = jnp.where(docs == 0, logs, -masked)
+
+    def earlier(at, carry):
+        acc_q[...] += step(at, base, None)
+        return carry
+
+    lax.fori_loop(0, block, earlier, 0)
+    lane = lax.broadcasted_iota(jnp.int32, (BLOCK, width), 1)
+    grad = jnp.where(lane < head_width, acc_q[:BLOCK, :], acc_q[BLOCK:, :])
+    gq_ref[...] = (grad * head_width**-0.5).astype(bf16)
+
+    @pl.when(block == pl.num_programs(0) - 1)
+    def _():
+        gk_ref[...] = acc_k[...].astype(bf16)
+        gv_ref[...] = acc_v[...].astype(bf16)
+
+
+def attend_plane_back(q, k, v, do, o, logs, doc_col, doc_row, head_width):
+    rows, width = q.shape
+    blocks = rows // BLOCK
+    whole = pl.BlockSpec((rows, width), lambda i: (0, 0))
+    part = pl.BlockSpec((BLOCK, width), lambda i: (i, 0))
+    return pl.pallas_call(
+        partial(attend_back_kernel, head_width),
+        grid=(blocks,),
+        out_shape=(jax.ShapeDtypeStruct((rows, width), bf16),) * 3,
+        in_specs=[
+            part,
+            whole,
+            whole,
+            part,
+            part,
+            pl.BlockSpec((1, 1, 2 * BLOCK), lambda i: (i, 0, 0)),
+            pl.BlockSpec((BLOCK, 1), lambda i: (i, 0)),
+            pl.BlockSpec((1, BLOCK), lambda i: (0, i)),
+        ],
+        out_specs=(part, whole, whole),
+        scratch_shapes=[
+            pltpu.VMEM((rows, width), f32),
+            pltpu.VMEM((rows, width), f32),
+            pltpu.VMEM((2 * BLOCK, width), f32),
+        ],
+        compiler_params=vmem_params(),
+    )(q, k, v, do, o, logs, doc_col, doc_row)
+
+
+def swap_core(values):
+    return lax.ppermute(values, "core", [(0, 1), (1, 0)])
+
+
+def by_core(own, other, core, axis):
+    lower = jnp.where(core == 0, own, other)
+    upper = jnp.where(core == 0, other, own)
+    return jnp.concatenate([lower, upper], axis=axis)
+
+
+def plane_device(
+    tokens,
+    segment_ids,
+    cotangent,
+    ln_attn_gain,
+    ln_attn_bias,
+    qkv_weight,
+    qv_bias,
+    head_scale,
+    out_weight,
+    out_bias,
+    ln_post_gain,
+    ln_post_bias,
+    ln_ffn_gain,
+    ln_ffn_bias,
+    fc1_weight,
+    fc1_bias,
+    mid_gain,
+    mid_bias,
+    fc2_weight,
+    fc2_bias,
+):
+    layers = qkv_weight.shape[0]
+    model_width = tokens.shape[1]
+    heads_all = head_scale.shape[1]
+    head_width = model_width // heads_all
+    hidden_here = fc1_weight.shape[2]
+    hidden_all = hidden_here * 8
+    quarter = hidden_here // 4
+    half_width = model_width // 2
+    x, y, core = lax.axis_index("x"), lax.axis_index("y"), lax.axis_index("core")
+    quarter_at = 2 * y + core
+    factor = head_width**-0.5
+
+    residual = to_plane(tokens).astype(f32)
+    docs = to_plane(segment_ids)
+    doc_col, doc_row = docs[:, None], docs[None, :]
+    gradient = to_plane(cotangent).astype(f32)
+
+    def own_heads(stacked):
+        return lax.dynamic_slice_in_dim(stacked, 2 * core, 2, 0)
+
+    def other_heads(stacked):
+        return lax.dynamic_slice_in_dim(stacked, 2 * (1 - core), 2, 0)
+
+    def cut(values, at, size, axis):
+        return lax.dynamic_slice_in_dim(values, at * size, size, axis)
+
+    def gather_attn(layer_index):
+        qkv = cut(cut(qkv_weight[layer_index], core, half_width, 0), y, head_width, 2)
+        stacked = lax.all_gather(qkv, "z", axis=0)
+        recv = swap_core(other_heads(stacked))
+        qkv = by_core(own_heads(stacked), recv, core, 1)
+        qkv = jnp.transpose(qkv, (1, 2, 0, 3)).reshape(model_width, 6 * head_width)
+        out = cut(cut(out_weight[layer_index], y, head_width, 0), core, half_width, 1)
+        stacked = lax.all_gather(out, "z", axis=0)
+        recv = swap_core(other_heads(stacked))
+        out = by_core(own_heads(stacked), recv, core, 2)
+        return qkv, out.reshape(2 * head_width, model_width)
+
+    def gather_ffn(layer_index):
+        first = cut(fc1_weight[layer_index], quarter_at, quarter, 1)
+        first = lax.all_gather(first, "z", axis=1, tiled=True)
+        second = cut(fc2_weight[layer_index], quarter_at, quarter, 0)
+        second = lax.all_gather(second, "z", axis=0, tiled=True)
+        return first, second
+
+    small = jnp.concatenate(
+        [
+            cut(qv_bias, y, head_width, 2).reshape(layers, 2 * head_width),
+            cut(fc1_bias, quarter_at, quarter, 1),
+            cut(mid_gain, quarter_at, quarter, 1),
+            cut(mid_bias, quarter_at, quarter, 1),
+        ],
+        axis=1,
+    )
+    small = lax.all_gather(small, "z", axis=0)
+    bias_heads = own_heads(small[:, :, : 2 * head_width]).reshape(2, layers, 2, head_width)
+    bias_heads = jnp.transpose(bias_heads, (1, 2, 0, 3)).reshape(layers, 2, 2 * head_width)
+
+    def hidden_rows(at):
+        first = 2 * head_width + at * quarter
+        part = small[:, :, first : first + quarter]
+        return jnp.transpose(part, (1, 0, 2)).reshape(layers, 4 * quarter)
+
+    shift_hidden, gain_hidden, bias_hidden = hidden_rows(0), hidden_rows(1), hidden_rows(2)
+    head_ids = ((2 * core + jnp.arange(2)) * 2 + x) * 2 + y
+    head_onehot = (head_ids[:, None] == jnp.arange(heads_all)[None, :]).astype(f32)
+
+    stored = []
+    for layer in range(layers):
+        qkv_here, out_here = gather_attn(layer)
+        first_here, second_here = gather_ffn(layer)
+        attn_in, attn_normal, attn_factor = norm_local(
+            residual, ln_attn_gain[layer], ln_attn_bias[layer]
+        )
+        attn_rows = plane_gather(attn_in.astype(bf16))
+        projected = jnp.dot(attn_rows, qkv_here, preferred_element_type=f32)
+        width = 2 * head_width
+        q = (projected[:, :width] + bias_heads[layer, 0]).astype(bf16) * factor
+        q = q.astype(bf16)
+        k = projected[:, width : 2 * width].astype(bf16)
+        v = (projected[:, 2 * width :] + bias_heads[layer, 1]).astype(bf16)
+        attended, logs = attend_plane(q, k, v, doc_col, doc_row, head_width)
+        scale = jnp.sum(head_onehot * head_scale[layer][None, :], axis=1)
+        scale_row = jnp.repeat(scale, head_width)[None, :]
+        scaled = (attended * scale_row).astype(bf16)
+        branch = plane_scatter(scaled, out_here, 0, 2) + out_bias[layer]
+        post_out, post_normal, post_factor = norm_local(
+            branch, ln_post_gain[layer], ln_post_bias[layer]
+        )
+        middle = residual + post_out
+        ffn_in, ffn_normal, ffn_factor = norm_local(middle, ln_ffn_gain[layer], ln_ffn_bias[layer])
+        ffn_rows = plane_gather(ffn_in.astype(bf16))
+        before = jnp.dot(ffn_rows, first_here, preferred_element_type=f32) + shift_hidden[layer]
+        activated = jax.nn.gelu(before, approximate=False)
+        sums = plane_sum(
+            jnp.stack([jnp.sum(activated, axis=1), jnp.sum(activated * activated, axis=1)])
+        )
+        average = sums[0] / hidden_all
+        spread = sums[1] / hidden_all - average * average
+        hidden_factor = lax.rsqrt(spread + epsilon)[:, None]
+        hidden_normal = (activated - average[:, None]) * hidden_factor
+        mixed = (hidden_normal * gain_hidden[layer] + bias_hidden[layer]).astype(bf16)
+        ffn_out = plane_scatter(mixed, second_here, 0, 3)
+        stored.append(
+            (
+                qkv_here,
+                out_here,
+                first_here,
+                second_here,
+                attn_normal,
+                attn_factor,
+                attn_rows,
+                q,
+                k,
+                v,
+                attended,
+                logs,
+                scale_row,
+                scaled,
+                post_normal,
+                post_factor,
+                ffn_normal,
+                ffn_factor,
+                ffn_rows,
+                before,
+                hidden_normal,
+                hidden_factor,
+                mixed,
+            )
+        )
+        residual = middle + ffn_out + fc2_bias[layer]
+    layer_output = from_plane(residual.astype(bf16))
+
+    def share_ffn(grad):
+        mine = lax.psum_scatter(grad.astype(bf16), "z", scatter_dimension=0, tiled=True)
+        return lax.all_gather(mine, ("y", "core"), axis=0, tiled=True).astype(f32)
+
+    def share_attn(grad):
+        grad = jnp.transpose(grad.astype(bf16), (1, 0, 2, 3))
+        own = cut(grad, core, half_width, 3)
+        recv = swap_core(cut(grad, 1 - core, half_width, 3))
+        stacked = by_core(own, recv, core, 0)
+        mine = lax.psum_scatter(stacked, "z", scatter_dimension=0)
+        full = lax.all_gather(mine, ("y", "core"), axis=0)
+        full = full.reshape(2, 2, 4, head_width, half_width).astype(f32)
+        qkv = jnp.transpose(full[:, :, :3], (1, 4, 2, 0, 3))
+        out = jnp.transpose(full[:, :, 3], (0, 2, 1, 3))
+        return (
+            qkv.reshape(model_width, 3, 2 * head_width),
+            out.reshape(2 * head_width, model_width),
+        )
+
+    big = [None] * layers
+    little = [None] * layers
+    for layer in reversed(range(layers)):
+        (
+            qkv_here,
+            out_here,
+            first_here,
+            second_here,
+            attn_normal,
+            attn_factor,
+            attn_rows,
+            q,
+            k,
+            v,
+            attended,
+            logs,
+            scale_row,
+            scaled,
+            post_normal,
+            post_factor,
+            ffn_normal,
+            ffn_factor,
+            ffn_rows,
+            before,
+            hidden_normal,
+            hidden_factor,
+            mixed,
+        ) = stored[layer]
+        second_shift_grad = jnp.sum(gradient, axis=0)
+        grad_rows = plane_gather(gradient.astype(bf16))
+        mixed_grad = jnp.einsum(
+            "td,fd->tf", grad_rows, second_here, preferred_element_type=f32
+        )
+        second_grad = share_ffn(
+            jnp.einsum("tf,td->fd", mixed, grad_rows, preferred_element_type=f32)
+        )
+        hidden_gain_grad = jnp.sum(mixed_grad * hidden_normal, axis=0)
+        hidden_shift_grad = jnp.sum(mixed_grad, axis=0)
+        normal_grad = mixed_grad * gain_hidden[layer]
+        sums = plane_sum(
+            jnp.stack(
+                [jnp.sum(normal_grad, axis=1), jnp.sum(normal_grad * hidden_normal, axis=1)]
+            )
+        )
+        active_grad = hidden_factor * (
+            normal_grad
+            - sums[0][:, None] / hidden_all
+            - hidden_normal * sums[1][:, None] / hidden_all
+        )
+        gelu_pull = jax.vjp(partial(jax.nn.gelu, approximate=False), before)[1]
+        pre_grad = gelu_pull(active_grad)[0].astype(bf16)
+        first_shift_grad = jnp.sum(pre_grad, axis=0, dtype=f32)
+        first_grad = share_ffn(
+            jnp.einsum("tf,td->fd", pre_grad, ffn_rows, preferred_element_type=f32)
+        ).T
+        ffn_in_grad = plane_scatter(pre_grad, first_here, 1, 4)
+        ffn_gain_grad = jnp.sum(ffn_in_grad * ffn_normal, axis=0)
+        ffn_bias_grad = jnp.sum(ffn_in_grad, axis=0)
+        middle_grad = gradient + norm_back(ffn_in_grad, ffn_normal, ffn_factor, ln_ffn_gain[layer])
+        post_gain_grad = jnp.sum(middle_grad * post_normal, axis=0)
+        post_bias_grad = jnp.sum(middle_grad, axis=0)
+        branch_grad = norm_back(middle_grad, post_normal, post_factor, ln_post_gain[layer])
+        out_shift_grad = jnp.sum(branch_grad, axis=0)
+        branch_rows = plane_gather(branch_grad.astype(bf16))
+        scaled_grad = jnp.einsum("td,cd->tc", branch_rows, out_here, preferred_element_type=f32)
+        out_grad = jnp.einsum("tc,td->cd", scaled, branch_rows, preferred_element_type=f32)
+        scale_cols = jnp.sum(attended * scaled_grad, axis=0)
+        scale_grad = jnp.sum(
+            head_onehot * jnp.sum(scale_cols.reshape(2, head_width), axis=1)[:, None], axis=0
+        )
+        attended_grad = (scaled_grad * scale_row).astype(bf16)
+        gq, gk, gv = attend_plane_back(
+            q, k, v, attended_grad, attended, logs, doc_col, doc_row, head_width
+        )
+        proj_grad = jnp.concatenate([gq, gk, gv], axis=1)
+        bias_grad = jnp.stack(
+            [jnp.sum(gq, axis=0, dtype=f32), jnp.sum(gv, axis=0, dtype=f32)], axis=0
+        )
+        qkv_grad = jnp.einsum("tc,td->cd", proj_grad, attn_rows, preferred_element_type=f32)
+        qkv_grad, out_grad = share_attn(
+            jnp.concatenate([qkv_grad, out_grad], axis=0).reshape(4, 2, head_width, model_width)
+        )
+        attn_in_grad = plane_scatter(proj_grad, qkv_here, 1, 5)
+        attn_gain_grad = jnp.sum(attn_in_grad * attn_normal, axis=0)
+        attn_bias_grad = jnp.sum(attn_in_grad, axis=0)
+        gradient = middle_grad + norm_back(
+            attn_in_grad, attn_normal, attn_factor, ln_attn_gain[layer]
+        )
+        big[layer] = (qkv_grad, out_grad, first_grad, second_grad)
+        hidden = jnp.stack([first_shift_grad, hidden_gain_grad, hidden_shift_grad])
+        hidden = lax.dynamic_update_slice(
+            jnp.zeros((3, 4, 2, 4, quarter), f32),
+            hidden.reshape(3, 4, 1, 1, quarter),
+            (0, 0, x, quarter_at, 0),
+        )
+        bias_grad = lax.dynamic_update_slice(
+            jnp.zeros((2, 4, 2, 2, head_width), f32),
+            bias_grad.reshape(2, 2, 1, 1, head_width),
+            (0, 2 * core, x, y, 0),
+        )
+        little[layer] = jnp.concatenate(
+            [
+                hidden.reshape(-1),
+                bias_grad.reshape(-1),
+                attn_gain_grad,
+                attn_bias_grad,
+                out_shift_grad,
+                post_gain_grad,
+                post_bias_grad,
+                ffn_gain_grad,
+                ffn_bias_grad,
+                second_shift_grad,
+                scale_grad,
+                jnp.zeros((-heads_all % 128,), f32),
+            ]
+        )
+    input_grad = from_plane(gradient.astype(bf16)).astype(f32)
+    stacked = lax.psum(jnp.stack(little), EVERY)
+    shard = 2 * lax.axis_index("z") + x
+    hidden = stacked[:, : 3 * hidden_all].reshape(layers, 3, 8, hidden_here)
+    hidden = lax.dynamic_index_in_dim(hidden, shard, 2, keepdims=False)
+    rest = stacked[:, 3 * hidden_all :]
+    bias_grad = rest[:, : 2 * model_width].reshape(layers, 2, 8, model_width // 8)
+    bias_grad = lax.dynamic_index_in_dim(bias_grad, shard, 2, keepdims=False)
+    rest = rest[:, 2 * model_width :]
+    vectors = [rest[:, i * model_width : (i + 1) * model_width] for i in range(8)]
+    scale_grad = rest[:, 8 * model_width : 8 * model_width + heads_all]
+    weights = [jnp.stack([big[layer][i] for layer in range(layers)]) for i in range(4)]
+    return (
+        layer_output,
+        input_grad,
+        vectors[0],
+        vectors[1],
+        weights[0],
+        bias_grad,
+        scale_grad,
+        weights[1],
+        vectors[2],
+        vectors[3],
+        vectors[4],
+        vectors[5],
+        vectors[6],
+        weights[2],
+        hidden[:, 0],
+        hidden[:, 1],
+        hidden[:, 2],
+        weights[3],
+        vectors[7],
+    )
+
+
+def split_specs(rows, mp):
+    both = tuple(rows) + tuple(mp)
+    in_specs = (
+        P(both, None),
+        P(rows),
+        P(both, None),
+        P(),
+        P(),
+        P(None, None, None, mp),
+        P(None, None, mp),
+        P(),
+        P(None, mp, None),
+        P(),
+        P(),
+        P(),
+        P(),
+        P(),
+        P(None, None, mp),
+        P(None, mp),
+        P(None, mp),
+        P(None, mp),
+        P(None, mp, None),
+        P(),
+    )
+    out_specs = (
+        P(both, None),
+        P(both, None),
+        P(),
+        P(),
+        P(None, None, None, mp),
+        P(None, None, mp),
+        P(),
+        P(None, mp, None),
+        P(),
+        P(),
+        P(),
+        P(),
+        P(),
+        P(None, None, mp),
+        P(None, mp),
+        P(None, mp),
+        P(None, mp),
+        P(None, mp, None),
+        P(),
+    )
+    return in_specs, out_specs
+
+
 def solution(mesh):
-    in_specs = (
-        P(("rows", "mp"), None),
-        P("rows"),
-        P(("rows", "mp"), None),
-        P(),
-        P(),
-        P(None, None, None, "mp"),
-        P(None, None, "mp"),
-        P(),
-        P(None, "mp", None),
-        P(),
-        P(),
-        P(),
-        P(),
-        P(),
-        P(None, None, "mp"),
-        P(None, "mp"),
-        P(None, "mp"),
-        P(None, "mp"),
-        P(None, "mp", None),
-        P(),
-    )
-    out_specs = (
-        P(("rows", "mp"), None),
-        P(("rows", "mp"), None),
-        P(),
-        P(),
-        P(None, None, None, "mp"),
-        P(None, None, "mp"),
-        P(),
-        P(None, "mp", None),
-        P(),
-        P(),
-        P(),
-        P(),
-        P(),
-        P(None, None, "mp"),
-        P(None, "mp"),
-        P(None, "mp"),
-        P(None, "mp"),
-        P(None, "mp", None),
-        P(),
-    )
+    if mesh.shape["rows"] == 4 and mesh.shape["mp"] == 8:
+        planes = Mesh(mesh.devices.reshape(2, 2, 4, 2), ("y", "core", "z", "x"))
+        in_specs, out_specs = split_specs(("y", "core"), ("z", "x"))
+        return jax.shard_map(
+            plane_device, mesh=planes, in_specs=in_specs, out_specs=out_specs, check_vma=False
+        )
+    in_specs, out_specs = split_specs(("rows",), ("mp",))
     return jax.shard_map(
         per_device, mesh=mesh, in_specs=in_specs, out_specs=out_specs, check_vma=False
     )

time: 2370 us -> 1170 us (0.49)
  waiting for transfers between devices: 1580 us -> 314 us
  Pallas kernels: 0 us -> 477 us
  matrix products: 265 us -> 79.9 us
  other arithmetic: 195 us -> 68.6 us
  local copies, waits for them, and re-layouts: 141 us -> 90 us
  blocking collectives: 121 us -> 85.4 us
  loops' own time: 31.7 us -> 0 us
    reduce_scatter x8 -> x6, waiting for transfers between devices: 718 us -> 57.8 us  [the longest x2 57.7 us: share_attn(): mine = lax.psum_scatter(stacked, 'z', scatter_dimension=0)]
    pallas_call x0 -> x24, Pallas kernels: none -> 477 us  [the longest x8 181 us: plane_gather(): pl.pallas_call(gather_kernel, out_shape=jax.ShapeDtypeStruct((8 * rows, w...]
    all_gather x8 -> x10, waiting for transfers between devices: 536 us -> 87.9 us  [the longest x4 57.8 us: share_ffn(): return lax.all_gather(mine, ('y', 'core'), axis=0, tiled=True).astype(f32)]
    dot_general x52 -> x16, matrix products: 265 us -> 79.9 us  [the longest x2 31.6 us: plane_device(): jnp.dot(ffn_rows, first_here, preferred_element_type=f32)]
    psum x5 -> x0, blocking collectives: 121 us -> none  [the longest x2 56.9 us: hidden_stats(): return lax.psum((first_sum, second_sum), 'mp')]
    psum x2 -> x1, waiting for transfers between devices: 222 us -> 128 us  [plane_device(): stacked = lax.psum(jnp.stack(little), EVERY)]
    all_gather x0 -> x5, blocking collectives: none -> 85.4 us  [the longest x2 47.8 us: gather_attn(): stacked = lax.all_gather(qkv, 'z', axis=0)]
    convert_element_type x29 -> x14, other arithmetic: 78.7 us -> 7.65 us  [the longest x2 3.04 us: share_attn(): full = full.reshape(2, 2, 4, head_width, half_width).astype(f32)]
  transfers between devices with their start and end apart: 34 -> 28, of which waited for: 32 -> 10; matrix products, arithmetic and copies ran while one was open for 4% -> 13% of each run, Pallas kernels for 0% -> 29%
where the time goes in v1:
time: 1170 us; the launch traced here: 1160 us
  Pallas kernels  477 us (41%)
  waiting for transfers between devices  314 us (27%)
  local copies, waits for them, and re-layouts  90 us (8%)
  blocking collectives  85.4 us (7%)
  matrix products  79.9 us (7%)
  other arithmetic  68.6 us (6%)
  starting transfers between devices  29.3 us (3%)
  between operations  17 us (1%)
    pallas_call x8, Pallas kernels, plane_gather(): pl.pallas_call(gather_kernel, out_shape=jax.ShapeDtypeStruct((8 * rows, w...  181 us
    pallas_call x8, Pallas kernels, plane_scatter(): pl.pallas_call(partial(scatter_kernel, weight_dim), out_shape=jax.ShapeDt...  180 us
    psum x1, waiting for transfers between devices, plane_device(): stacked = lax.psum(jnp.stack(little), EVERY)  128 us
    all_gather x4, waiting for transfers between devices, share_ffn(): return lax.all_gather(mine, ('y', 'core'), axis=0, tiled=True).astype(f32)  57.8 us
    reduce_scatter x2, waiting for transfers between devices, share_attn(): mine = lax.psum_scatter(stacked, 'z', scatter_dimension=0)  57.7 us
    all_gather x2, blocking collectives, gather_attn(): stacked = lax.all_gather(qkv, 'z', axis=0)  47.8 us
    pallas_call x2, Pallas kernels, attend_plane_back(): pl.pallas_call(partial(attend_back_kernel, head_width), grid=(blocks,), o...  47.7 us
    pallas_call x2, Pallas kernels, attend_plane(): pl.pallas_call(partial(attend_kernel, head_width), grid=(blocks,), out_sh...  46.6 us
  transfers between devices with their start and end apart: 28, of which 10 were waited for; matrix products, arithmetic and copies ran while one was open for 13% of the time, Pallas kernels for 29%

profile of v1, /device:TPU:1, one launch (start us, length us, event | category | flops | bytes accessed | tf_op | source)
XLA Modules:
  0.0 1160.7 jit_solution(4592289612777671374)
XLA Ops:
  15.7 29.4 %all_gather.52 = bf16[4,512,3,64]{1,3,0,2:T(8,128)(2,1)S(1)} all-gather(bf16[1,512,3,64]{1,3,0,2:T(8,128)(2,1)S(1)} %copy.167), channel_id=1, replica_groups=mesh['y'=2,'core'=2,'z'=4,'x'=2] {'z'}, dimensions={0}, use_global_device_ids=true | all-gather | bytes 983040 | tf_op jit(solution)/shard_map/all_gather | solution.py:1052
  138.4 37.8 %collective-permute-done = bf16[256,1024]{1,0:T(8,128)(2,1)S(1)} collective-permute-done((bf16[256,1024]{1,0:T(8,128)(2,1)}, bf16[256,1024]{1,0:T(8,128)(2,1)S(1)}, u32[]{:S(2)}, u32[]{:S(2)}) %collective-permute-start) | collective-permute-done | bytes 524320 | tf_op jit(solution)/shard_map/ppermute | solution.py:540
  176.9 22.9 %shard_map.339 = bf16[2048,1024]{1,0:T(8,128)(2,1)S(1)} custom-call(bf16[256,1024]{1,0:T(8,128)(2,1)S(1)} %fusion.21.x_ref), custom_call_target="tpu_custom_call" | custom-call | tf_op jit(solution)/shard_map/pallas_call | solution.py:611
  202.5 23.3 %shard_map.340 = (f32[2048,128]{1,0:T(8,128)S(1)}, f32[8,1,512]{2,1,0:T(1,128)S(1)}) custom-call(bf16[2048,128]{1,0:T(8,128)(2,1)S(1)} %get-tuple-element.218.q_ref, bf16[2048,128]{1,0:T(8,128)(2,1)S(1)} %get-tuple-element.217.k_ref, bf16[2048,128]{1,0:T(8,128)(2,1)S(1)} %fusion.31.v_ref, s32[2048,1]{1,0:T(8,128)S(1)} %copy.141.dq_ref.dcol_ref, ...), custom_call_target="tpu_custom_call" | custom-call | tf_op jit(solution)/shard_map/pallas_call | solution.py:863
  226.8 22.4 %shard_map.341 = f32[256,1024]{1,0:T(8,128)S(1)} custom-call(bf16[2048,128]{1,0:T(8,128)(2,1)S(1)} %multiply_convert_fusion.3.a_ref, bf16[128,1024]{1,0:T(8,128)(2,1)S(1)} %bitcast.208), custom_call_target="tpu_custom_call" | custom-call | tf_op jit(solution)/shard_map/pallas_call | solution.py:724
  252.0 22.6 %shard_map.342 = bf16[2048,1024]{1,0:T(8,128)(2,1)S(1)} custom-call(bf16[256,1024]{1,0:T(8,128)(2,1)S(1)} %add_convert_fusion.7.x_ref), custom_call_target="tpu_custom_call" | custom-call | tf_op jit(solution)/shard_map/pallas_call | solution.py:611
  276.6 22.8 %shard_map.351 = bf16[2048,1024]{1,0:T(8,128)(2,1)S(1)} custom-call(bf16[256,1024]{1,0:T(8,128)(2,1)S(1)} %collective-permute-done.7.x_ref), custom_call_target="tpu_custom_call" | custom-call | tf_op jit(solution)/shard_map/pallas_call | solution.py:611
  326.6 22.8 %shard_map.344 = f32[256,1024]{1,0:T(8,128)S(1)} custom-call(bf16[2048,512]{1,0:T(8,128)(2,1)S(1)} %copy-done.11, bf16[512,1024]{1,0:T(8,128)(2,1)S(1)} %bitcast.213), custom_call_target="tpu_custom_call" | custom-call | tf_op jit(solution)/shard_map/pallas_call | solution.py:724
  350.2 22.8 %shard_map.345 = bf16[2048,1024]{1,0:T(8,128)(2,1)S(1)} custom-call(bf16[256,1024]{1,0:T(8,128)(2,1)S(1)} %add_convert_fusion.6.x_ref), custom_call_target="tpu_custom_call" | custom-call | tf_op jit(solution)/shard_map/pallas_call | solution.py:611
  375.7 23.3 %shard_map.346 = (f32[2048,128]{1,0:T(8,128)S(1)}, f32[8,1,512]{2,1,0:T(1,128)S(1)}) custom-call(bf16[2048,128]{1,0:T(8,128)(2,1)S(1)} %get-tuple-element.216.q_ref, bf16[2048,128]{1,0:T(8,128)(2,1)S(1)} %get-tuple-element.215.k_ref, bf16[2048,128]{1,0:T(8,128)(2,1)S(1)} %fusion.29.v_ref, s32[2048,1]{1,0:T(8,128)S(1)} %copy.141.dq_ref.dcol_ref, ...), custom_call_target="tpu_custom_call" | custom-call | tf_op jit(solution)/shard_map/pallas_call | solution.py:863
  424.2 22.5 %shard_map.348 = bf16[2048,1024]{1,0:T(8,128)(2,1)S(1)} custom-call(bf16[256,1024]{1,0:T(8,128)(2,1)S(1)} %add_convert_fusion.5.x_ref), custom_call_target="tpu_custom_call" | custom-call | tf_op jit(solution)/shard_map/pallas_call | solution.py:611
  508.2 22.8 %shard_map.353 = f32[256,1024]{1,0:T(8,128)S(1)} custom-call(bf16[2048,512]{1,0:T(8,128)(2,1)S(1)} %copy-done.10, bf16[1024,512]{1,0:T(8,128)(2,1)S(1)} %bitcast.214), custom_call_target="tpu_custom_call" | custom-call | tf_op jit(solution)/shard_map/pallas_call | solution.py:724
  531.7 22.9 %shard_map.350 = f32[256,1024]{1,0:T(8,128)S(1)} custom-call(bf16[2048,512]{1,0:T(8,128)(2,1)S(1)} %copy-done.7, bf16[512,1024]{1,0:T(8,128)(2,1)S(1)} %bitcast.215), custom_call_target="tpu_custom_call" | custom-call | tf_op jit(solution)/shard_map/pallas_call | solution.py:724
  556.9 22.7 %shard_map.354 = bf16[2048,1024]{1,0:T(8,128)(2,1)S(1)} custom-call(bf16[256,1024]{1,0:T(8,128)(2,1)S(1)} %get-tuple-element.199.x_ref), custom_call_target="tpu_custom_call" | custom-call | tf_op jit(solution)/shard_map/pallas_call | solution.py:611
  583.5 24.1 %shard_map.355 = (bf16[2048,128]{1,0:T(8,128)(2,1)S(1)}, bf16[2048,128]{1,0:T(8,128)(2,1)S(1)}, bf16[2048,128]{1,0:T(8,128)(2,1)S(1)}) custom-call(bf16[2048,128]{1,0:T(8,128)(2,1)S(1)} %copy-done.28, bf16[2048,128]{1,0:T(8,128)(2,1)S(1)} %copy-done.26, bf16[2048,128]{1,0:T(8,128)(2,1)S(1)} %copy-done.20, bf16[2048,128]{1,0:T(8,128)(2,1)S(1)} %get-tuple-element.238.do_ref, ...), custom_call_target="tpu_custom_call" | custom-call | tf_op jit(solution)/shard_map/pallas_call | solution.py:968
  607.9 22.5 %shard_map.356 = f32[256,1024]{1,0:T(8,128)S(1)} custom-call(bf16[2048,384]{1,0:T(8,128)(2,1)S(1)} %constant_dynamic-update-slice_fusion.a_ref, bf16[1024,384]{1,0:T(8,128)(2,1)S(1)} %copy-done.42), custom_call_target="tpu_custom_call" | custom-call | tf_op jit(solution)/shard_map/pallas_call | solution.py:724
  631.6 22.5 %shard_map.357 = bf16[2048,1024]{1,0:T(8,128)(2,1)S(1)} custom-call(bf16[256,1024]{1,0:T(8,128)(2,1)S(1)} %convert_element_type.148.x_ref), custom_call_target="tpu_custom_call" | custom-call | tf_op jit(solution)/shard_map/pallas_call | solution.py:611
  677.6 22.2 %shard_map.359 = f32[256,1024]{1,0:T(8,128)S(1)} custom-call(bf16[2048,512]{1,0:T(8,128)(2,1)S(1)} %get-tuple-element.197.a_ref, bf16[1024,512]{1,0:T(8,128)(2,1)S(1)} %bitcast.212), custom_call_target="tpu_custom_call" | custom-call | tf_op jit(solution)/shard_map/pallas_call | solution.py:724
  707.6 22.6 %shard_map.360 = bf16[2048,1024]{1,0:T(8,128)(2,1)S(1)} custom-call(bf16[256,1024]{1,0:T(8,128)(2,1)S(1)} %get-tuple-element.195.x_ref), custom_call_target="tpu_custom_call" | custom-call | tf_op jit(solution)/shard_map/pallas_call | solution.py:611
  731.5 23.6 %shard_map.361 = (bf16[2048,128]{1,0:T(8,128)(2,1)S(1)}, bf16[2048,128]{1,0:T(8,128)(2,1)S(1)}, bf16[2048,128]{1,0:T(8,128)(2,1)S(1)}) custom-call(bf16[2048,128]{1,0:T(8,128)(2,1)S(1)} %copy-done.24, bf16[2048,128]{1,0:T(8,128)(2,1)S(1)} %copy-done.22, bf16[2048,128]{1,0:T(8,128)(2,1)S(1)} %copy-done.18, bf16[2048,128]{1,0:T(8,128)(2,1)S(1)} %get-tuple-element.240.do_ref, ...), custom_call_target="tpu_custom_call" | custom-call | tf_op jit(solution)/shard_map/pallas_call | solution.py:968
  783.9 22.6 %shard_map.362 = f32[256,1024]{1,0:T(8,128)S(1)} custom-call(bf16[2048,384]{1,0:T(8,128)(2,1)S(1)} %constant_dynamic-update-slice_fusion.3.a_ref, bf16[1024,384]{1,0:T(8,128)(2,1)S(1)} %copy-done.41), custom_call_target="tpu_custom_call" | custom-call | tf_op jit(solution)/shard_map/pallas_call | solution.py:724
  820.2 27.9 %reduce-scatter.7.cloned.1.call-done = bf16[1,4,64,512]{3,2,1,0:T(8,128)(2,1)} async-done(((bf16[4,4,64,512]{3,2,1,0:T(8,128)(2,1)}), bf16[1,4,64,512]{3,2,1,0:T(8,128)(2,1)}) %reduce-scatter.7.cloned.1.call-update) | async-done | bytes 262160 | tf_op jit(solution)/shard_map/reduce_scatter | solution.py:1166
  857.1 128.1 %all-reduce.2.cloned.1.call-done = f32[2,22656]{1,0:T(2,128)} async-done(((f32[2,22656]{1,0:T(2,128)}), f32[2,22656]{1,0:T(2,128)}) %all-reduce.2.cloned.1.call-update) | async-done | bytes 181264 | tf_op jit(solution)/shard_map/psum | solution.py:1293
  986.8 29.8 %reduce-scatter.9.cloned.1.call-done = bf16[1,4,64,512]{3,2,1,0:T(8,128)(2,1)} async-done(((bf16[4,4,64,512]{3,2,1,0:T(8,128)(2,1)}), bf16[1,4,64,512]{3,2,1,0:T(8,128)(2,1)}) %reduce-scatter.9.cloned.1.call-update) | async-done | bytes 262160 | tf_op jit(solution)/shard_map/reduce_scatter | solution.py:1166
  (569 shorter events, 456.9 us)
Async XLA Ops:
  7.2 294.2 %all-gather.29.cloned.1.call-start = ((), (), s32[]{:S(2)}) async-start(), calls=%async_computation.19 | async-start | bytes 1310720 | tf_op jit(solution)/shard_map/all_gather | solution.py:1064
  10.8 313.0 %all-gather.31.cloned.1.call-start = ((), (), s32[]{:S(2)}) async-start(), calls=%async_computation.20 | async-start | bytes 1310720 | tf_op jit(solution)/shard_map/all_gather | solution.py:1066
  11.8 436.9 %all-gather.33.cloned.1.call-start = ((), (), s32[]{:S(2)}) async-start(), calls=%async_computation.21 | async-start | bytes 1310720 | tf_op jit(solution)/shard_map/all_gather | solution.py:1064
  13.6 456.3 %all-gather.35.cloned.1.call-start = ((), (), s32[]{:S(2)}) async-start(), calls=%async_computation.22 | async-start | bytes 1310720 | tf_op jit(solution)/shard_map/all_gather | solution.py:1066
  45.8 82.7 %collective-permute-start.1 = (bf16[2,512,3,64]{1,3,0,2:T(8,128)(2,1)}, bf16[2,512,3,64]{1,3,0,2:T(8,128)(2,1)}, u32[]{:S(2)}, u32[]{:S(2)}) collective-permute-start(bf16[2,512,3,64]{1,3,0,2:T(8,128)(2,1)} %constant_dynamic-slice_fusion.21), channel_id=1, source_target_pairs={{0,8},{8,0},{1,9},{9,1},{2,10},{10,2},{3,11},{11,3},{4,12},{12,4},... | collective-permute-start | bytes 1179656 | tf_op jit(solution)/shard_map/ppermute | solution.py:993
  67.3 61.2 %collective-permute-start.4 = (bf16[2,512,3,64]{1,3,0,2:T(8,128)(2,1)}, bf16[2,512,3,64]{1,3,0,2:T(8,128)(2,1)}, u32[]{:S(2)}, u32[]{:S(2)}) collective-permute-start(bf16[2,512,3,64]{1,3,0,2:T(8,128)(2,1)} %constant_dynamic-slice_fusion.10), channel_id=1, source_target_pairs={{0,8},{8,0},{1,9},{9,1},{2,10},{10,2},{3,11},{11,3},{4,12},{12,4},... | collective-permute-start | bytes 1179656 | tf_op jit(solution)/shard_map/ppermute | solution.py:993
  69.5 50.0 %collective-permute-start.2 = (s32[2048]{0:T(1024)S(1)}, s32[2048]{0:T(1024)S(1)}, u32[]{:S(2)}, u32[]{:S(2)}) collective-permute-start(s32[2048]{0:T(1024)S(1)} %copy-done.132), channel_id=1, source_target_pairs={{0,0},{1,1},{2,16},{3,17},{4,8},{5,9},{6,24},{7,25},{8,2},{9,3},{1... | collective-permute-start | bytes 24584 | tf_op jit(solution)/shard_map/ppermute | solution.py:540
  105.8 711.9 %reduce-scatter.13.cloned.1.call-start = ((), (), s32[]{:S(2)}) async-start(), calls=%async_computation.13 | async-start | bytes 1310720 | tf_op jit(solution)/shard_map/reduce_scatter | solution.py:1158
  119.5 56.7 %collective-permute-start = (bf16[256,1024]{1,0:T(8,128)(2,1)}, bf16[256,1024]{1,0:T(8,128)(2,1)S(1)}, u32[]{:S(2)}, u32[]{:S(2)}) collective-permute-start(bf16[256,1024]{1,0:T(8,128)(2,1)} %param.20), channel_id=1, source_target_pairs={{0,0},{1,1},{2,16},{3,17},{4,8},{5,9},{6,24},{7,25},{8,2},{9,3},{1... | collective-permute-start | bytes 1572872 | tf_op jit(solution)/shard_map/ppermute | solution.py:540
  126.0 150.6 %collective-permute-start.7 = (bf16[256,1024]{1,0:T(8,128)(2,1)}, bf16[256,1024]{1,0:T(8,128)(2,1)S(1)}, u32[]{:S(2)}, u32[]{:S(2)}) collective-permute-start(bf16[256,1024]{1,0:T(8,128)(2,1)} %param.22), channel_id=1, source_target_pairs={{0,0},{1,1},{2,16},{3,17},{4,8},{5,9},{6,24},{7,25},{8,2},{9,3},{1... | collective-permute-start | bytes 1572872 | tf_op jit(solution)/shard_map/ppermute | solution.py:540
  656.1 162.3 %reduce-scatter.11.cloned.1.call-start = ((), (), s32[]{:S(2)}) async-start(), calls=%async_computation.11 | async-start | bytes 1310720 | tf_op jit(solution)/shard_map/reduce_scatter | solution.py:1158
  705.8 113.3 %reduce-scatter.15.cloned.1.call-start = ((), (), s32[]{:S(2)}) async-start(), calls=%async_computation.15 | async-start | bytes 1310720 | tf_op jit(solution)/shard_map/reduce_scatter | solution.py:1158
  762.5 57.1 %reduce-scatter.17.cloned.1.call-start = ((), (), s32[]{:S(2)}) async-start(), calls=%async_computation.17 | async-start | bytes 1310720 | tf_op jit(solution)/shard_map/reduce_scatter | solution.py:1158
  776.0 72.1 %reduce-scatter.7.cloned.1.call-start = ((), (), s32[]{:S(2)}) async-start(), calls=%async_computation.7 | async-start | bytes 1310720 | tf_op jit(solution)/shard_map/reduce_scatter | solution.py:1166
  814.5 170.7 %all-reduce.2.cloned.1.call-start = ((), (), s32[]{:S(2)}) async-start(), calls=%async_computation.6 | async-start | bytes 362496 | tf_op jit(solution)/shard_map/psum | solution.py:1293
  815.4 201.2 %reduce-scatter.9.cloned.1.call-start = ((), (), s32[]{:S(2)}) async-start(), calls=%async_computation.9 | async-start | bytes 1310720 | tf_op jit(solution)/shard_map/reduce_scatter | solution.py:1166
  817.7 216.3 %all-gather.23.cloned.1.call-start = ((), (), s32[]{:S(2)}) async-start(), calls=%async_computation.14 | async-start | bytes 1310720 | tf_op jit(solution)/shard_map/all_gather | solution.py:1159
  818.3 234.0 %all-gather.21.cloned.1.call-start = ((), (), s32[]{:S(2)}) async-start(), calls=%async_computation.12 | async-start | bytes 1310720 | tf_op jit(solution)/shard_map/all_gather | solution.py:1159
  819.0 251.5 %all-gather.25.cloned.1.call-start = ((), (), s32[]{:S(2)}) async-start(), calls=%async_computation.16 | async-start | bytes 1310720 | tf_op jit(solution)/shard_map/all_gather | solution.py:1159
  819.6 269.1 %all-gather.27.cloned.1.call-start = ((), (), s32[]{:S(2)}) async-start(), calls=%async_computation.18 | async-start | bytes 1310720 | tf_op jit(solution)/shard_map/all_gather | solution.py:1159
  820.2 286.6 %all-gather.17.cloned.1.call-start = ((), (), s32[]{:S(2)}) async-start(), calls=%async_computation.8 | async-start | bytes 1310720 | tf_op jit(solution)/shard_map/all_gather | solution.py:1167
  848.2 276.8 %all-gather.19.cloned.1.call-start = ((), (), s32[]{:S(2)}) async-start(), calls=%async_computation.10 | async-start | bytes 1310720 | tf_op jit(solution)/shard_map/all_gather | solution.py:1167
  848.7 171.9 %collective-permute-start.8 = (bf16[256,1024]{1,0:T(8,128)(2,1)S(1)}, bf16[256,1024]{1,0:T(8,128)(2,1)S(1)}, u32[]{:S(2)}, u32[]{:S(2)}) collective-permute-start(bf16[256,1024]{1,0:T(8,128)(2,1)S(1)} %fusion.26), channel_id=1, source_target_pairs={{0,0},{1,1},{16,2},{17,3},{8,4},{9,5},{24,6},{25,7},{2,8},{3,9},{1... | collective-permute-start | bytes 1572872 | tf_op jit(solution)/shard_map/ppermute | solution.py:544
  852.1 169.6 %collective-permute-start.6 = (bf16[256,1024]{1,0:T(8,128)(2,1)}, bf16[256,1024]{1,0:T(8,128)(2,1)S(1)}, u32[]{:S(2)}, u32[]{:S(2)}) collective-permute-start(bf16[256,1024]{1,0:T(8,128)(2,1)} %get-tuple-element.241), channel_id=1, source_target_pairs={{0,0},{1,1},{16,2},{17,3},{8,4},{9,5},{24,6},{25,7},{2,8},{3,9},{1... | collective-permute-start | bytes 1572872 | tf_op jit(solution)/shard_map/ppermute | solution.py:544
  (137 other events, 4244.3 us)
Sparse Core Ops, SparseCore 0:
  10.9 41.6 all-gather.28
  54.2 34.1 all-gather.30
  90.0 31.5 all-gather.32
  123.1 51.0 all-gather.34
  656.2 27.8 reduce-scatter.12
  705.9 28.3 reduce-scatter.10
  762.7 27.9 reduce-scatter.14
  793.6 25.7 reduce-scatter.16
  822.3 25.7 reduce-scatter.6
  854.5 130.6 all-reduce.1
  988.2 28.4 reduce-scatter.8
  1018.0 15.9 all-gather.22
  1035.6 16.7 all-gather.20
  1053.7 16.7 all-gather.24
  1071.9 16.7 all-gather.26
  1090.1 16.7 all-gather.16
  1108.2 16.7 all-gather.18

commit v2 on v1

--- a/solution.py
+++ b/solution.py
@@ -544,189 +544,182 @@
     return lax.ppermute(values, EVERY, [(target, source) for source, target in plane_pairs()])
 
 
-def greet(peers):
-    barrier = pltpu.get_barrier_semaphore()
-    for peer in peers:
-        pl.semaphore_signal(barrier, inc=1, device_id=peer, device_id_type=MESH_ID)
-    pl.semaphore_wait(barrier, len(peers))
-
-
-def gather_kernel(x_ref, o_ref, send_sem, recv_sem, own_sem):
-    rows = x_ref.shape[0]
-    half = rows // 2
-    x, y, core = lax.axis_index("x"), lax.axis_index("y"), lax.axis_index("core")
-    to_x, to_y, to_core = {"x": 1 - x}, {"y": 1 - y}, {"core": 1 - core}
-    greet((to_x, to_y, to_core))
-
-    def place(at_x, at_y, part=None):
-        first = ((2 * core + at_y) * 2 + at_x) * rows
+class Here:
+    def __init__(self):
+        self.x, self.y = lax.axis_index("x"), lax.axis_index("y")
+        self.core, self.z = lax.axis_index("core"), lax.axis_index("z")
+
+    def peer(self, flip_x, flip_y, flip_core, step_z):
+        place = {}
+        if flip_x:
+            place["x"] = 1 - self.x
+        if flip_y:
+            place["y"] = 1 - self.y
+        if flip_core:
+            place["core"] = 1 - self.core
+        if step_z:
+            place["z"] = lax.rem(self.z + step_z, 4)
+        return place
+
+
+BY_X, BY_Y, BY_CORE = (1, 0, 0, 0), (0, 1, 0, 0), (0, 0, 1, 0)
+BY_Z = tuple((0, 0, 0, step) for step in (1, 2, 3))
+BY_LINE = BY_Z + tuple((0, 0, 1, step) for step in range(4))
+BY_PLANE = tuple((flip & 1, flip >> 1 & 1, flip >> 2, 0) for flip in range(1, 8))
+
+
+def remote(source, target, send_sem, recv_sem, place):
+    return pltpu.make_async_remote_copy(
+        src_ref=source,
+        dst_ref=target,
+        send_sem=send_sem,
+        recv_sem=recv_sem,
+        device_id=place,
+        device_id_type=MESH_ID,
+    )
+
+
+def dma_sems(count):
+    return pltpu.SemaphoreType.DMA((count,))
+
+
+class Task:
+    arrays = ()
+    spaces = ()
+    outs = ()
+    out_spaces = ()
+    scratch = ()
+    reach = ()
+
+    def start(self, here, ins, outs, scratch):
+        pass
+
+    def finish(self, here, ins, outs, scratch):
+        pass
+
+
+def run_tasks(ids, *tasks):
+    reach = []
+    for task in tasks:
+        reach += [way for way in task.reach if way not in reach]
+
+    def kernel(*refs):
+        refs = list(refs)
+        views = [[], [], []]
+        for kind, name in enumerate(("arrays", "outs", "scratch")):
+            for task in tasks:
+                count = len(getattr(task, name))
+                views[kind].append(refs[:count])
+                refs = refs[count:]
+        here = Here()
+        barrier = pltpu.get_barrier_semaphore()
+        for way in reach:
+            pl.semaphore_signal(barrier, inc=1, device_id=here.peer(*way), device_id_type=MESH_ID)
+        pl.semaphore_wait(barrier, len(reach))
+        for task, *held in zip(tasks, *views):
+            task.start(here, *held)
+        for task, *held in zip(tasks, *views):
+            task.finish(here, *held)
+
+    results = pl.pallas_call(
+        kernel,
+        out_shape=[out for task in tasks for out in task.outs],
+        in_specs=[pl.BlockSpec(memory_space=s) for task in tasks for s in task.spaces],
+        out_specs=[pl.BlockSpec(memory_space=s) for task in tasks for s in task.out_spaces],
+        scratch_shapes=[each for task in tasks for each in task.scratch],
+        compiler_params=vmem_params(next(ids)),
+    )(*[array for task in tasks for array in task.arrays])
+    results = list(results)
+    split = []
+    for task in tasks:
+        split.append(results[: len(task.outs)])
+        results = results[len(task.outs) :]
+    return split
+
+
+class PlaneGather(Task):
+    def __init__(self, block):
+        rows, width = block.shape
+        self.arrays, self.spaces = (block,), (pltpu.VMEM,)
+        self.outs = (jax.ShapeDtypeStruct((8 * rows, width), block.dtype),)
+        self.out_spaces = (pltpu.VMEM,)
+        self.scratch = (dma_sems(11), dma_sems(11), pltpu.SemaphoreType.DMA)
+        self.reach = (BY_X, BY_Y, BY_CORE)
+
+    def place(self, here, o_ref, at_x, at_y, part=None):
+        rows = o_ref.shape[0] // 8
+        first = ((2 * here.core + at_y) * 2 + at_x) * rows
         if part is None:
             return o_ref.at[pl.ds(pl.multiple_of(first, rows), rows)]
+        half = rows // 2
         return o_ref.at[pl.ds(pl.multiple_of(first + part * half, half), half)]
 
-    def copy(index, source, target, peer):
-        return pltpu.make_async_remote_copy(
-            src_ref=source,
-            dst_ref=target,
-            send_sem=send_sem.at[index],
-            recv_sem=recv_sem.at[index],
-            device_id=peer,
-            device_id_type=MESH_ID,
-        )
-
-    own = place(x, y)
-    copy_0 = copy(0, x_ref, own, to_x)
-    copy_1 = copy(1, x_ref, own, to_y)
-    copy_2 = copy(2, x_ref, own, to_core)
-    copy_0.start()
-    copy_1.start()
-    copy_2.start()
-    keep = pltpu.make_async_copy(x_ref, own, own_sem)
-    keep.start()
-    copy_0.wait_recv()
-    copy_4 = copy(4, place(1 - x, y, 0), place(1 - x, y, 0), to_y)
-    copy_3 = copy(3, place(1 - x, y), place(1 - x, y), to_core)
-    copy_4.start()
-    copy_3.start()
-    copy_1.wait_recv()
-    copy_6 = copy(6, place(x, 1 - y, 1), place(x, 1 - y, 1), to_x)
-    copy_5 = copy(5, place(x, 1 - y), place(x, 1 - y), to_core)
-    copy_6.start()
-    copy_5.start()
-    copy_4.wait_recv()
-    copy_7 = copy(7, place(1 - x, 1 - y, 0), place(1 - x, 1 - y, 0), to_core)
-    copy_7.start()
-    copy_6.wait_recv()
-    copy_8 = copy(8, place(1 - x, 1 - y, 1), place(1 - x, 1 - y, 1), to_core)
-    copy_8.start()
-    for arriving in (copy_2, copy_3, copy_5, copy_7, copy_8):
-        arriving.wait_recv()
-    for sent in (copy_0, copy_1, copy_2, copy_3, copy_4, copy_5, copy_6, copy_7, copy_8):
-        sent.wait_send()
-    keep.wait()
-
-
-def plane_gather(block_b):
-    rows, width = block_b.shape
-    return pl.pallas_call(
-        gather_kernel,
-        out_shape=jax.ShapeDtypeStruct((8 * rows, width), block_b.dtype),
-        in_specs=[pl.BlockSpec(memory_space=pltpu.VMEM)],
-        out_specs=pl.BlockSpec(memory_space=pltpu.VMEM),
-        scratch_shapes=[
-            pltpu.SemaphoreType.DMA((9,)),
-            pltpu.SemaphoreType.DMA((9,)),
-            pltpu.SemaphoreType.DMA,
-        ],
-        compiler_params=vmem_params(1),
-    )(block_b)
-
-
-def scatter_kernel(
-    weight_dim,
-    a_ref,
-    w_ref,
-    o_ref,
-    sib_out,
-    sib_in,
-    diag_out,
-    diag_in,
-    last_x_out,
-    last_y_out,
-    last_x_in,
-    last_y_in,
-    wait_x,
-    wait_y,
-    send_sem,
-    recv_sem,
-):
-    rows = o_ref.shape[0]
-    half = rows // 2
-    x, y, core = lax.axis_index("x"), lax.axis_index("y"), lax.axis_index("core")
-    to_x, to_y, to_core = {"x": 1 - x}, {"y": 1 - y}, {"core": 1 - core}
-    greet((to_x, to_y, to_core))
-
-    def term(at_core, at_x, at_y):
-        first = pl.multiple_of(((2 * at_core + at_y) * 2 + at_x) * rows, rows)
-        return lax.dot_general(
-            a_ref[pl.ds(first, rows), :],
-            w_ref[...],
-            (((1,), (weight_dim,)), ((), ())),
-            preferred_element_type=f32,
-        )
-
-    def copy(index, source, target, peer):
-        return pltpu.make_async_remote_copy(
-            src_ref=source,
-            dst_ref=target,
-            send_sem=send_sem.at[index],
-            recv_sem=recv_sem.at[index],
-            device_id=peer,
-            device_id_type=MESH_ID,
-        )
-
-    places = ((1 - x, 1 - y), (1 - x, y), (x, 1 - y), (x, y))
-    siblings = [copy(i, sib_out.at[i], sib_in.at[i], to_core) for i in range(4)]
-
-    def help_sibling(i):
-        sib_out[i] = term(1 - core, *places[i]).astype(bf16)
-        siblings[i].start()
-
-    def joined(i):
-        mine = term(core, *places[i])
-        siblings[i].wait_recv()
-        return mine + sib_in[i].astype(f32)
-
-    help_sibling(0)
-    help_sibling(1)
-    total = joined(0)
-    diag_out[...] = total.astype(bf16)
-    diag_x = copy(4, diag_out.at[pl.ds(0, half)], diag_in.at[0], to_x)
-    diag_y = copy(5, diag_out.at[pl.ds(half, half)], diag_in.at[1], to_y)
-    diag_x.start()
-    diag_y.start()
-    help_sibling(2)
-    total = joined(1)
-    last_x_out[0] = total[:half].astype(bf16)
-    x_0 = copy(6, last_x_out.at[0], last_x_in.at[0], to_x)
-    x_0.start()
-    wait_x[...] = total[half:]
-    help_sibling(3)
-    total = joined(2)
-    last_y_out[1] = total[half:].astype(bf16)
-    y_1 = copy(7, last_y_out.at[1], last_y_in.at[1], to_y)
-    y_1.start()
-    wait_y[...] = total[:half]
-    diag_y.wait_recv()
-    last_x_out[1] = (wait_x[...] + diag_in[1].astype(f32)).astype(bf16)
-    x_1 = copy(8, last_x_out.at[1], last_x_in.at[1], to_x)
-    x_1.start()
-    diag_x.wait_recv()
-    last_y_out[0] = (wait_y[...] + diag_in[0].astype(f32)).astype(bf16)
-    y_0 = copy(9, last_y_out.at[0], last_y_in.at[0], to_y)
-    y_0.start()
-    o_ref[...] = joined(3)
-    x_0.wait_recv()
-    y_1.wait_recv()
-    x_1.wait_recv()
-    y_0.wait_recv()
-    for part in range(2):
-        piece = pl.ds(part * half, half)
-        o_ref[piece, :] += last_x_in[part].astype(f32) + last_y_in[part].astype(f32)
-    for sent in (*siblings, diag_x, diag_y, x_0, y_1, x_1, y_0):
-        sent.wait_send()
-
-
-def plane_scatter(operand_b, weight_b, weight_dim, collective_id):
-    rows = operand_b.shape[0] // 8
-    half = rows // 2
-    width = weight_b.shape[1 - weight_dim]
-    return pl.pallas_call(
-        partial(scatter_kernel, weight_dim),
-        out_shape=jax.ShapeDtypeStruct((rows, width), f32),
-        in_specs=[pl.BlockSpec(memory_space=pltpu.VMEM)] * 2,
-        out_specs=pl.BlockSpec(memory_space=pltpu.VMEM),
-        scratch_shapes=[
+    def copies(self, here, x_ref, o_ref, send_sem, recv_sem):
+        x, y = here.x, here.y
+        half = x_ref.shape[0] // 2
+        to_x, to_y, to_core = here.peer(*BY_X), here.peer(*BY_Y), here.peer(*BY_CORE)
+
+        def copy(index, source, target, way):
+            return remote(source, target, send_sem.at[index], recv_sem.at[index], way)
+
+        def pass_on(index, way, *at):
+            return copy(index, self.place(here, o_ref, *at), self.place(here, o_ref, *at), way)
+
+        own = [self.place(here, o_ref, x, y, part) for part in (0, 1)]
+        mine = [x_ref.at[pl.ds(part * half, half)] for part in (0, 1)]
+        return [
+            copy(0, mine[0], own[0], to_x),
+            copy(1, mine[1], own[1], to_y),
+            copy(2, mine[1], own[1], to_x),
+            copy(3, mine[0], own[0], to_y),
+            copy(4, x_ref, self.place(here, o_ref, x, y), to_core),
+            pass_on(5, to_y, 1 - x, y, 0),
+            pass_on(6, to_x, x, 1 - y, 1),
+            pass_on(7, to_core, 1 - x, y),
+            pass_on(8, to_core, x, 1 - y),
+            pass_on(9, to_core, 1 - x, 1 - y, 0),
+            pass_on(10, to_core, 1 - x, 1 - y, 1),
+        ]
+
+    def keep(self, here, x_ref, o_ref, own_sem):
+        return pltpu.make_async_copy(x_ref, self.place(here, o_ref, here.x, here.y), own_sem)
+
+    def start(self, here, ins, outs, scratch):
+        copies = self.copies(here, ins[0], outs[0], scratch[0], scratch[1])
+        for index in range(5):
+            copies[index].start()
+        self.keep(here, ins[0], outs[0], scratch[2]).start()
+
+    def finish(self, here, ins, outs, scratch):
+        copies = self.copies(here, ins[0], outs[0], scratch[0], scratch[1])
+        copies[0].wait_recv()
+        copies[5].start()
+        copies[1].wait_recv()
+        copies[6].start()
+        copies[2].wait_recv()
+        copies[7].start()
+        copies[3].wait_recv()
+        copies[8].start()
+        copies[5].wait_recv()
+        copies[9].start()
+        copies[6].wait_recv()
+        copies[10].start()
+        for index in (4, 7, 8, 9, 10):
+            copies[index].wait_recv()
+        for each in copies:
+            each.wait_send()
+        self.keep(here, ins[0], outs[0], scratch[2]).wait()
+
+
+class PlaneScatter(Task):
+    def __init__(self, operand, weight, weight_dim):
+        rows = operand.shape[0] // 8
+        half = rows // 2
+        width = weight.shape[1 - weight_dim]
+        self.weight_dim = weight_dim
+        self.arrays, self.spaces = (operand, weight), (pltpu.VMEM,) * 2
+        self.outs, self.out_spaces = (jax.ShapeDtypeStruct((rows, width), f32),), (pltpu.VMEM,)
+        self.scratch = (
             pltpu.VMEM((4, rows, width), bf16),
             pltpu.VMEM((4, rows, width), bf16),
             pltpu.VMEM((rows, width), bf16),
@@ -737,60 +730,365 @@
             pltpu.VMEM((2, half, width), bf16),
             pltpu.VMEM((half, width), f32),
             pltpu.VMEM((half, width), f32),
-            pltpu.SemaphoreType.DMA((10,)),
-            pltpu.SemaphoreType.DMA((10,)),
-        ],
-        compiler_params=vmem_params(collective_id),
-    )(operand_b, weight_b)
-
-
-def plane_sum_kernel(v_ref, o_ref, got, send_sem, recv_sem):
-    x, y, core = lax.axis_index("x"), lax.axis_index("y"), lax.axis_index("core")
-    peers = []
-    for flip in range(1, 8):
-        at_x = 1 - x if flip & 1 else x
-        at_y = 1 - y if flip & 2 else y
-        at_core = 1 - core if flip & 4 else core
-        peers.append({"x": at_x, "y": at_y, "core": at_core})
-    greet(peers)
-    me = (2 * core + y) * 2 + x
-    copies = []
-    for index, peer in enumerate(peers):
-        copies.append(
-            pltpu.make_async_remote_copy(
-                src_ref=v_ref,
-                dst_ref=got.at[index],
-                send_sem=send_sem.at[index],
-                recv_sem=recv_sem.at[index],
-                device_id=peer,
-                device_id_type=MESH_ID,
+            dma_sems(10),
+            dma_sems(10),
+        )
+        self.reach = (BY_X, BY_Y, BY_CORE)
+
+    def rows_of(self, ins, first, rows):
+        return ins[0][pl.ds(first, rows), :]
+
+    def finish(self, here, ins, outs, scratch):
+        w_ref, o_ref = ins[1], outs[0]
+        (
+            sib_out,
+            sib_in,
+            diag_out,
+            diag_in,
+            last_x_out,
+            last_y_out,
+            last_x_in,
+            last_y_in,
+            wait_x,
+            wait_y,
+            send_sem,
+            recv_sem,
+        ) = scratch
+        rows = o_ref.shape[0]
+        half = rows // 2
+        x, y, core = here.x, here.y, here.core
+        to_x, to_y, to_core = here.peer(*BY_X), here.peer(*BY_Y), here.peer(*BY_CORE)
+
+        def term(at_core, at_x, at_y):
+            first = pl.multiple_of(((2 * at_core + at_y) * 2 + at_x) * rows, rows)
+            return lax.dot_general(
+                self.rows_of(ins, first, rows),
+                w_ref[...],
+                (((1,), (self.weight_dim,)), ((), ())),
+                preferred_element_type=f32,
             )
-        )
-    for each in copies:
-        each.start()
-    for each in copies:
-        each.wait_recv()
-    by_x = [v_ref[...] + got[0]]
-    for flip in (2, 4, 6):
-        by_x.append(got[flip - 1] + got[flip])
-    o_ref[...] = (by_x[0] + by_x[1]) + (by_x[2] + by_x[3])
-    for each in copies:
-        each.wait_send()
-
-
-def plane_sum(values):
-    return pl.pallas_call(
-        plane_sum_kernel,
-        out_shape=jax.ShapeDtypeStruct(values.shape, f32),
-        in_specs=[pl.BlockSpec(memory_space=pltpu.VMEM)],
-        out_specs=pl.BlockSpec(memory_space=pltpu.VMEM),
-        scratch_shapes=[
-            pltpu.VMEM((7, *values.shape), f32),
-            pltpu.SemaphoreType.DMA((7,)),
-            pltpu.SemaphoreType.DMA((7,)),
-        ],
-        compiler_params=vmem_params(6),
-    )(values)
+
+        def copy(index, source, target, way):
+            return remote(source, target, send_sem.at[index], recv_sem.at[index], way)
+
+        places = ((1 - x, 1 - y), (1 - x, y), (x, 1 - y), (x, y))
+        siblings = [copy(i, sib_out.at[i], sib_in.at[i], to_core) for i in range(4)]
+
+        def help_sibling(i):
+            sib_out[i] = term(1 - core, *places[i]).astype(bf16)
+            siblings[i].start()
+
+        def joined(i):
+            mine = term(core, *places[i])
+            siblings[i].wait_recv()
+            return mine + sib_in[i].astype(f32)
+
+        help_sibling(0)
+        help_sibling(1)
+        total = joined(0)
+        diag_out[...] = total.astype(bf16)
+        diag_x = copy(4, diag_out.at[pl.ds(0, half)], diag_in.at[0], to_x)
+        diag_y = copy(5, diag_out.at[pl.ds(half, half)], diag_in.at[1], to_y)
+        diag_x.start()
+        diag_y.start()
+        help_sibling(2)
+        total = joined(1)
+        last_x_out[0] = total[:half].astype(bf16)
+        x_0 = copy(6, last_x_out.at[0], last_x_in.at[0], to_x)
+        x_0.start()
+        wait_x[...] = total[half:]
+        total = joined(2)
+        last_y_out[1] = total[half:].astype(bf16)
+        y_1 = copy(7, last_y_out.at[1], last_y_in.at[1], to_y)
+        y_1.start()
+        wait_y[...] = total[:half]
+        help_sibling(3)
+        diag_y.wait_recv()
+        last_x_out[1] = (wait_x[...] + diag_in[1].astype(f32)).astype(bf16)
+        x_1 = copy(8, last_x_out.at[1], last_x_in.at[1], to_x)
+        x_1.start()
+        diag_x.wait_recv()
+        last_y_out[0] = (wait_y[...] + diag_in[0].astype(f32)).astype(bf16)
+        y_0 = copy(9, last_y_out.at[0], last_y_in.at[0], to_y)
+        y_0.start()
+        o_ref[...] = joined(3)
+        for part, (by_x, by_y) in enumerate(((x_0, y_0), (x_1, y_1))):
+            by_x.wait_recv()
+            by_y.wait_recv()
+            piece = pl.ds(part * half, half)
+            o_ref[piece, :] += last_x_in[part].astype(f32) + last_y_in[part].astype(f32)
+        for sent in (*siblings, diag_x, diag_y, x_0, y_1, x_1, y_0):
+            sent.wait_send()
+
+
+class PlaneSum(Task):
+    def __init__(self, values):
+        self.arrays, self.spaces = (values,), (pltpu.VMEM,)
+        self.outs = (jax.ShapeDtypeStruct(values.shape, f32),)
+        self.out_spaces = (pltpu.VMEM,)
+        self.scratch = (pltpu.VMEM((7, *values.shape), f32), dma_sems(7), dma_sems(7))
+        self.reach = BY_PLANE
+
+    def copies(self, here, ins, scratch):
+        got, send_sem, recv_sem = scratch
+        return [
+            remote(ins[0], got.at[i], send_sem.at[i], recv_sem.at[i], here.peer(*way))
+            for i, way in enumerate(BY_PLANE)
+        ]
+
+    def start(self, here, ins, outs, scratch):
+        for each in self.copies(here, ins, scratch):
+            each.start()
+
+    def finish(self, here, ins, outs, scratch):
+        copies = self.copies(here, ins, scratch)
+        for each in copies:
+            each.wait_recv()
+        got = scratch[0]
+        by_x = [ins[0][...] + got[0]]
+        for flip in (2, 4, 6):
+            by_x.append(got[flip - 1] + got[flip])
+        outs[0][...] = (by_x[0] + by_x[1]) + (by_x[2] + by_x[3])
+        for each in copies:
+            each.wait_send()
+
+
+class LineGather(Task):
+    def __init__(self, values):
+        self.arrays, self.spaces = (values,), (pl.ANY,)
+        self.outs = (jax.ShapeDtypeStruct((4, *values.shape), values.dtype),)
+        self.out_spaces = (pl.ANY,)
+        self.scratch = (dma_sems(4), dma_sems(3))
+        self.reach = BY_Z
+
+    def copies(self, here, ins, outs, scratch):
+        target = outs[0].at[here.z]
+        keep = pltpu.make_async_copy(ins[0], target, scratch[0].at[3])
+        return keep, [
+            remote(ins[0], target, scratch[0].at[i], scratch[1].at[i], here.peer(*way))
+            for i, way in enumerate(BY_Z)
+        ]
+
+    def start(self, here, ins, outs, scratch):
+        keep, copies = self.copies(here, ins, outs, scratch)
+        for each in copies:
+            each.start()
+        keep.start()
+
+    def finish(self, here, ins, outs, scratch):
+        keep, copies = self.copies(here, ins, outs, scratch)
+        for each in copies:
+            each.wait()
+        keep.wait()
+
+
+class HeadGather(Task):
+    def __init__(self, values):
+        kinds, wide, half = values.shape
+        self.arrays, self.spaces = (values,), (pl.ANY,)
+        self.outs = (jax.ShapeDtypeStruct((kinds, 2, wide, 2 * half), values.dtype),)
+        self.out_spaces = (pl.ANY,)
+        self.scratch = (dma_sems(4), dma_sems(4))
+        self.reach = BY_LINE
+
+    def piece(self, outs, shard, part):
+        half = outs[0].shape[3] // 2
+        return outs[0].at[:, shard, :, pl.ds(pl.multiple_of(part * half, half), half)]
+
+    def copies(self, here, ins, outs, scratch):
+        shard, target_core = lax.rem(here.z, 2), here.z // 2
+        target = self.piece(outs, shard, here.core)
+        recv_sem = scratch[1].at[2 * shard + here.core]
+        keep = pltpu.make_async_copy(ins[0], target, recv_sem)
+        return keep, [
+            remote(
+                ins[0],
+                target,
+                scratch[0].at[step],
+                recv_sem,
+                {"core": target_core, "z": lax.rem(here.z + step, 4)},
+            )
+            for step in range(4)
+        ]
+
+    def start(self, here, ins, outs, scratch):
+        keep, copies = self.copies(here, ins, outs, scratch)
+        for each in copies[1:]:
+            each.start()
+        at_home = here.z // 2 == here.core
+        pl.when(at_home)(keep.start)
+        pl.when(jnp.logical_not(at_home))(copies[0].start)
+
+    def finish(self, here, ins, outs, scratch):
+        keep, copies = self.copies(here, ins, outs, scratch)
+        for shard in range(2):
+            for part in range(2):
+                piece = self.piece(outs, shard, part)
+                pltpu.make_async_copy(piece, piece, scratch[1].at[2 * shard + part]).wait()
+        for each in copies[1:]:
+            each.wait_send()
+        pl.when(here.z // 2 != here.core)(copies[0].wait_send)
+
+
+class LineScatter(Task):
+    def __init__(self, values):
+        shape = values.shape[1:]
+        self.arrays, self.spaces = (values,), (pltpu.VMEM,)
+        self.outs, self.out_spaces = (jax.ShapeDtypeStruct(shape, values.dtype),), (pltpu.VMEM,)
+        self.scratch = (pltpu.VMEM((3, *shape), values.dtype), dma_sems(3), dma_sems(3))
+        self.reach = BY_Z
+
+    def copies(self, here, ins, scratch):
+        got, send_sem, recv_sem = scratch
+        return [
+            remote(
+                ins[0].at[lax.rem(here.z + i + 1, 4)],
+                got.at[i],
+                send_sem.at[i],
+                recv_sem.at[i],
+                here.peer(*way),
+            )
+            for i, way in enumerate(BY_Z)
+        ]
+
+    def start(self, here, ins, outs, scratch):
+        for each in self.copies(here, ins, scratch):
+            each.start()
+
+    def finish(self, here, ins, outs, scratch):
+        copies = self.copies(here, ins, scratch)
+        for each in copies:
+            each.wait_recv()
+        total = ins[0][here.z].astype(f32)
+        for i in range(3):
+            total = total + scratch[0][i].astype(f32)
+        outs[0][...] = total.astype(outs[0].dtype)
+        for each in copies:
+            each.wait_send()
+
+
+class HeadScatter(Task):
+    def __init__(self, values):
+        kinds, _, wide, width = values.shape
+        shape = (kinds, wide, width // 2)
+        self.arrays, self.spaces = (values,), (pltpu.VMEM,)
+        self.outs, self.out_spaces = (jax.ShapeDtypeStruct(shape, values.dtype),), (pltpu.VMEM,)
+        self.scratch = (pltpu.VMEM((4, *shape), values.dtype), dma_sems(4), dma_sems(4))
+        self.reach = BY_LINE
+
+    def copies(self, here, ins, scratch):
+        got, send_sem, recv_sem = scratch
+        half = ins[0].shape[3] // 2
+        triples = []
+        for shard in range(2):
+            for part in range(2):
+                source = ins[0].at[:, shard, :, pl.ds(part * half, half)]
+                target_z = 2 * here.core + shard
+                slot = recv_sem.at[here.z]
+                away = remote(
+                    source,
+                    got.at[here.z],
+                    send_sem.at[2 * shard + part],
+                    slot,
+                    {"core": part, "z": target_z},
+                )
+                stay = pltpu.make_async_copy(source, got.at[here.z], slot)
+                at_home = (target_z == here.z) & (here.core == part)
+                triples.append((away, stay, at_home))
+        return triples
+
+    def start(self, here, ins, outs, scratch):
+        for away, stay, at_home in self.copies(here, ins, scratch):
+            pl.when(at_home)(stay.start)
+            pl.when(jnp.logical_not(at_home))(away.start)
+
+    def finish(self, here, ins, outs, scratch):
+        got, send_sem, recv_sem = scratch
+        for plane in range(4):
+            pltpu.make_async_copy(got.at[plane], got.at[plane], recv_sem.at[plane]).wait()
+        total = got[0].astype(f32)
+        for plane in range(1, 4):
+            total = total + got[plane].astype(f32)
+        outs[0][...] = total.astype(outs[0].dtype)
+        for away, stay, at_home in self.copies(here, ins, scratch):
+            pl.when(jnp.logical_not(at_home))(away.wait_send)
+
+
+class RowsGather(Task):
+    def __init__(self, values):
+        self.arrays, self.spaces = (values,), (pl.ANY,)
+        self.outs = (jax.ShapeDtypeStruct((4, *values.shape), values.dtype),)
+        self.out_spaces = (pl.ANY,)
+        self.scratch = (dma_sems(4), dma_sems(3))
+        self.reach = (BY_Y, BY_CORE)
+
+    def copies(self, here, ins, outs, scratch):
+        send_sem, recv_sem = scratch
+        own = outs[0].at[2 * here.y + here.core]
+        over = outs[0].at[2 * (1 - here.y) + here.core]
+        to_y, to_core = here.peer(*BY_Y), here.peer(*BY_CORE)
+        return (
+            pltpu.make_async_copy(ins[0], own, send_sem.at[3]),
+            remote(ins[0], own, send_sem.at[0], recv_sem.at[0], to_y),
+            remote(ins[0], own, send_sem.at[1], recv_sem.at[1], to_core),
+            remote(over, over, send_sem.at[2], recv_sem.at[2], to_core),
+        )
+
+    def start(self, here, ins, outs, scratch):
+        keep, by_y, by_core, again = self.copies(here, ins, outs, scratch)
+        by_y.start()
+        by_core.start()
+        keep.start()
+
+    def finish(self, here, ins, outs, scratch):
+        keep, by_y, by_core, again = self.copies(here, ins, outs, scratch)
+        by_y.wait_recv()
+        again.start()
+        by_core.wait_recv()
+        again.wait_recv()
+        for each in (by_y, by_core, again):
+            each.wait_send()
+        keep.wait()
+
+
+class PlaneThenLineSum(Task):
+    def __init__(self, values, ready):
+        rows, width = values.shape
+        both = (rows + ready.shape[0], width)
+        self.plane = PlaneSum(values)
+        self.arrays, self.spaces = (values, ready), (pltpu.VMEM,) * 2
+        self.outs, self.out_spaces = (jax.ShapeDtypeStruct(both, f32),), (pltpu.VMEM,)
+        self.scratch = (
+            *self.plane.scratch,
+            pltpu.VMEM((4, *both), f32),
+            pltpu.VMEM(both, f32),
+            dma_sems(3),
+            dma_sems(4),
+        )
+        self.reach = BY_PLANE + BY_Z
+
+    def start(self, here, ins, outs, scratch):
+        self.plane.start(here, ins[:1], None, scratch[:3])
+
+    def finish(self, here, ins, outs, scratch):
+        got, mine, send_sem, recv_sem = scratch[3:]
+        rows = ins[0].shape[0]
+        first = ins[1].shape[0]
+        self.plane.finish(here, ins[:1], (mine.at[pl.ds(first, rows)],), scratch[:3])
+        mine[:first, :] = ins[1][...]
+        copies = [
+            remote(mine, got.at[here.z], send_sem.at[i], recv_sem.at[here.z], here.peer(*way))
+            for i, way in enumerate(BY_Z)
+        ]
+        for each in copies:
+            each.start()
+        keep = pltpu.make_async_copy(mine, got.at[here.z], recv_sem.at[here.z])
+        keep.start()
+        for plane in range(4):
+            pltpu.make_async_copy(got.at[plane], got.at[plane], recv_sem.at[plane]).wait()
+        outs[0][...] = (got[0] + got[1]) + (got[2] + got[3])
+        for each in copies:
+            each.wait_send()
 
 
 BLOCK = 256
@@ -987,16 +1285,6 @@
         ],
         compiler_params=vmem_params(),
     )(q, k, v, do, o, logs, doc_col, doc_row)
-
-
-def swap_core(values):
-    return lax.ppermute(values, "core", [(0, 1), (1, 0)])
-
-
-def by_core(own, other, core, axis):
-    lower = jnp.where(core == 0, own, other)
-    upper = jnp.where(core == 0, other, own)
-    return jnp.concatenate([lower, upper], axis=axis)
 
 
 def plane_device(
@@ -1038,34 +1326,16 @@
     doc_col, doc_row = docs[:, None], docs[None, :]
     gradient = to_plane(cotangent).astype(f32)
 
-    def own_heads(stacked):
-        return lax.dynamic_slice_in_dim(stacked, 2 * core, 2, 0)
-
-    def other_heads(stacked):
-        return lax.dynamic_slice_in_dim(stacked, 2 * (1 - core), 2, 0)
-
     def cut(values, at, size, axis):
         return lax.dynamic_slice_in_dim(values, at * size, size, axis)
 
-    def gather_attn(layer_index):
-        qkv = cut(cut(qkv_weight[layer_index], core, half_width, 0), y, head_width, 2)
-        stacked = lax.all_gather(qkv, "z", axis=0)
-        recv = swap_core(other_heads(stacked))
-        qkv = by_core(own_heads(stacked), recv, core, 1)
-        qkv = jnp.transpose(qkv, (1, 2, 0, 3)).reshape(model_width, 6 * head_width)
-        out = cut(cut(out_weight[layer_index], y, head_width, 0), core, half_width, 1)
-        stacked = lax.all_gather(out, "z", axis=0)
-        recv = swap_core(other_heads(stacked))
-        out = by_core(own_heads(stacked), recv, core, 2)
-        return qkv, out.reshape(2 * head_width, model_width)
-
-    def gather_ffn(layer_index):
-        first = cut(fc1_weight[layer_index], quarter_at, quarter, 1)
-        first = lax.all_gather(first, "z", axis=1, tiled=True)
-        second = cut(fc2_weight[layer_index], quarter_at, quarter, 0)
-        second = lax.all_gather(second, "z", axis=0, tiled=True)
-        return first, second
-
+    head_parts, first_parts, second_parts = [], [], []
+    for layer in range(layers):
+        qkv = cut(cut(qkv_weight[layer], core, half_width, 0), y, head_width, 2)
+        out = cut(cut(out_weight[layer], y, head_width, 0), core, half_width, 1)
+        head_parts.append(jnp.concatenate([jnp.transpose(qkv, (1, 2, 0)), out[None]], axis=0))
+        first_parts.append(cut(fc1_weight[layer], quarter_at, quarter, 1).T)
+        second_parts.append(cut(fc2_weight[layer], quarter_at, quarter, 0))
     small = jnp.concatenate(
         [
             cut(qv_bias, y, head_width, 2).reshape(layers, 2 * head_width),
@@ -1075,29 +1345,56 @@
         ],
         axis=1,
     )
-    small = lax.all_gather(small, "z", axis=0)
-    bias_heads = own_heads(small[:, :, : 2 * head_width]).reshape(2, layers, 2, head_width)
-    bias_heads = jnp.transpose(bias_heads, (1, 2, 0, 3)).reshape(layers, 2, 2 * head_width)
-
-    def hidden_rows(at):
-        first = 2 * head_width + at * quarter
-        part = small[:, :, first : first + quarter]
-        return jnp.transpose(part, (1, 0, 2)).reshape(layers, 4 * quarter)
-
-    shift_hidden, gain_hidden, bias_hidden = hidden_rows(0), hidden_rows(1), hidden_rows(2)
     head_ids = ((2 * core + jnp.arange(2)) * 2 + x) * 2 + y
     head_onehot = (head_ids[:, None] == jnp.arange(heads_all)[None, :]).astype(f32)
+    width = 2 * head_width
+    heads_here, first_here, second_here = [None] * layers, [None] * layers, [None] * layers
+
+    ids = iter(range(1, 64))
+
+    def plane_sum(values):
+        return run_tasks(ids, PlaneSum(values))[0][0]
 
     stored = []
     for layer in range(layers):
-        qkv_here, out_here = gather_attn(layer)
-        first_here, second_here = gather_ffn(layer)
         attn_in, attn_normal, attn_factor = norm_local(
             residual, ln_attn_gain[layer], ln_attn_bias[layer]
         )
-        attn_rows = plane_gather(attn_in.astype(bf16))
-        projected = jnp.dot(attn_rows, qkv_here, preferred_element_type=f32)
-        width = 2 * head_width
+        if layer == 0:
+            ((attn_rows,), (heads_here[0],), (small,)) = run_tasks(
+                ids, PlaneGather(attn_in.astype(bf16)), HeadGather(head_parts[0]), LineGather(small)
+            )
+            bias_heads = lax.dynamic_slice_in_dim(small[:, :, :width], 2 * core, 2, 0)
+            bias_heads = jnp.transpose(
+                bias_heads.reshape(2, layers, 2, head_width), (1, 2, 0, 3)
+            ).reshape(layers, 2, width)
+
+            def hidden_rows(at):
+                part = small[:, :, width + at * quarter : width + (at + 1) * quarter]
+                return jnp.transpose(part, (1, 0, 2)).reshape(layers, 4 * quarter)
+
+            shift_hidden, gain_hidden, bias_hidden = map(hidden_rows, range(3))
+            beside = [(first_parts, first_here, 0), (second_parts, second_here, 0)]
+            beside += [(head_parts, heads_here, 1)]
+        else:
+            ((attn_rows,), (first,)) = run_tasks(
+                ids, PlaneGather(attn_in.astype(bf16)), LineGather(first_parts[layer])
+            )
+            first_here[layer] = first.reshape(4 * quarter, model_width)
+            beside = [(second_parts, second_here, 1), None, None]
+        qkv_here = heads_here[layer][:3].reshape(3 * width, model_width)
+        out_here = heads_here[layer][3].reshape(width, model_width)
+
+        def with_weights(main, item):
+            if item is None:
+                return run_tasks(ids, main)[0][0]
+            parts, here_list, at = item
+            kind = HeadGather if parts is head_parts else LineGather
+            ((result,), (got,)) = run_tasks(ids, main, kind(parts[at]))
+            here_list[at] = got if kind is HeadGather else got.reshape(4 * quarter, model_width)
+            return result
+
+        projected = jnp.einsum("td,cd->tc", attn_rows, qkv_here, preferred_element_type=f32)
         q = (projected[:, :width] + bias_heads[layer, 0]).astype(bf16) * factor
         q = q.astype(bf16)
         k = projected[:, width : 2 * width].astype(bf16)
@@ -1106,14 +1403,18 @@
         scale = jnp.sum(head_onehot * head_scale[layer][None, :], axis=1)
         scale_row = jnp.repeat(scale, head_width)[None, :]
         scaled = (attended * scale_row).astype(bf16)
-        branch = plane_scatter(scaled, out_here, 0, 2) + out_bias[layer]
+        branch = with_weights(PlaneScatter(scaled, out_here, 0), beside[0])
+        branch = branch + out_bias[layer]
         post_out, post_normal, post_factor = norm_local(
             branch, ln_post_gain[layer], ln_post_bias[layer]
         )
         middle = residual + post_out
         ffn_in, ffn_normal, ffn_factor = norm_local(middle, ln_ffn_gain[layer], ln_ffn_bias[layer])
-        ffn_rows = plane_gather(ffn_in.astype(bf16))
-        before = jnp.dot(ffn_rows, first_here, preferred_element_type=f32) + shift_hidden[layer]
+        ffn_rows = with_weights(
+            PlaneGather(ffn_in.astype(bf16)), beside[1]
+        )
+        before = jnp.einsum("td,fd->tf", ffn_rows, first_here[layer], preferred_element_type=f32)
+        before = before + shift_hidden[layer]
         activated = jax.nn.gelu(before, approximate=False)
         sums = plane_sum(
             jnp.stack([jnp.sum(activated, axis=1), jnp.sum(activated * activated, axis=1)])
@@ -1123,13 +1424,13 @@
         hidden_factor = lax.rsqrt(spread + epsilon)[:, None]
         hidden_normal = (activated - average[:, None]) * hidden_factor
         mixed = (hidden_normal * gain_hidden[layer] + bias_hidden[layer]).astype(bf16)
-        ffn_out = plane_scatter(mixed, second_here, 0, 3)
+        ffn_out = with_weights(
+            PlaneScatter(mixed, second_here[layer], 0), beside[2]
+        )
         stored.append(
             (
                 qkv_here,
                 out_here,
-                first_here,
-                second_here,
                 attn_normal,
                 attn_factor,
                 attn_rows,
@@ -1154,18 +1455,14 @@
         residual = middle + ffn_out + fc2_bias[layer]
     layer_output = from_plane(residual.astype(bf16))
 
-    def share_ffn(grad):
-        mine = lax.psum_scatter(grad.astype(bf16), "z", scatter_dimension=0, tiled=True)
-        return lax.all_gather(mine, ("y", "core"), axis=0, tiled=True).astype(f32)
-
-    def share_attn(grad):
-        grad = jnp.transpose(grad.astype(bf16), (1, 0, 2, 3))
-        own = cut(grad, core, half_width, 3)
-        recv = swap_core(cut(grad, 1 - core, half_width, 3))
-        stacked = by_core(own, recv, core, 0)
-        mine = lax.psum_scatter(stacked, "z", scatter_dimension=0)
-        full = lax.all_gather(mine, ("y", "core"), axis=0)
-        full = full.reshape(2, 2, 4, head_width, half_width).astype(f32)
+    def by_shard(grad):
+        return grad.astype(bf16).reshape(4, quarter, model_width)
+
+    def ffn_shard(grad):
+        return grad.reshape(4 * quarter, model_width).astype(f32)
+
+    def head_shard(grad):
+        full = grad.reshape(2, 2, 4, head_width, half_width).astype(f32)
         qkv = jnp.transpose(full[:, :, :3], (1, 4, 2, 0, 3))
         out = jnp.transpose(full[:, :, 3], (0, 2, 1, 3))
         return (
@@ -1173,14 +1470,15 @@
             out.reshape(2 * head_width, model_width),
         )
 
-    big = [None] * layers
-    little = [None] * layers
+    pending = None
+    first_done, second_done = [None] * layers, [None] * layers
+    heads_done, hidden_done = [None] * layers, [None] * layers
+    vector_grads = [None] * layers
+    norm_grads = []
     for layer in reversed(range(layers)):
         (
             qkv_here,
             out_here,
-            first_here,
-            second_here,
             attn_normal,
             attn_factor,
             attn_rows,
@@ -1202,13 +1500,14 @@
             mixed,
         ) = stored[layer]
         second_shift_grad = jnp.sum(gradient, axis=0)
-        grad_rows = plane_gather(gradient.astype(bf16))
+        sides = [] if pending is None else [RowsGather(each) for each in pending]
+        ((grad_rows,), *got) = run_tasks(ids, PlaneGather(gradient.astype(bf16)), *sides)
+        if pending is not None:
+            heads_done[layer + 1], hidden_done[layer + 1] = got[0][0], got[1][0]
         mixed_grad = jnp.einsum(
-            "td,fd->tf", grad_rows, second_here, preferred_element_type=f32
-        )
-        second_grad = share_ffn(
-            jnp.einsum("tf,td->fd", mixed, grad_rows, preferred_element_type=f32)
-        )
+            "td,fd->tf", grad_rows, second_here[layer], preferred_element_type=f32
+        )
+        second_grad = jnp.einsum("tf,td->fd", mixed, grad_rows, preferred_element_type=f32)
         hidden_gain_grad = jnp.sum(mixed_grad * hidden_normal, axis=0)
         hidden_shift_grad = jnp.sum(mixed_grad, axis=0)
         normal_grad = mixed_grad * gain_hidden[layer]
@@ -1225,10 +1524,10 @@
         gelu_pull = jax.vjp(partial(jax.nn.gelu, approximate=False), before)[1]
         pre_grad = gelu_pull(active_grad)[0].astype(bf16)
         first_shift_grad = jnp.sum(pre_grad, axis=0, dtype=f32)
-        first_grad = share_ffn(
-            jnp.einsum("tf,td->fd", pre_grad, ffn_rows, preferred_element_type=f32)
-        ).T
-        ffn_in_grad = plane_scatter(pre_grad, first_here, 1, 4)
+        first_grad = jnp.einsum("tf,td->fd", pre_grad, ffn_rows, preferred_element_type=f32)
+        ((ffn_in_grad,), (second_grad,)) = run_tasks(
+            ids, PlaneScatter(pre_grad, first_here[layer], 0), LineScatter(by_shard(second_grad))
+        )
         ffn_gain_grad = jnp.sum(ffn_in_grad * ffn_normal, axis=0)
         ffn_bias_grad = jnp.sum(ffn_in_grad, axis=0)
         middle_grad = gradient + norm_back(ffn_in_grad, ffn_normal, ffn_factor, ln_ffn_gain[layer])
@@ -1236,7 +1535,13 @@
         post_bias_grad = jnp.sum(middle_grad, axis=0)
         branch_grad = norm_back(middle_grad, post_normal, post_factor, ln_post_gain[layer])
         out_shift_grad = jnp.sum(branch_grad, axis=0)
-        branch_rows = plane_gather(branch_grad.astype(bf16))
+        ((branch_rows,), (first_grad,), (second_grad,)) = run_tasks(
+            ids,
+            PlaneGather(branch_grad.astype(bf16)),
+            LineScatter(by_shard(first_grad)),
+            RowsGather(second_grad),
+        )
+        second_done[layer] = second_grad
         scaled_grad = jnp.einsum("td,cd->tc", branch_rows, out_here, preferred_element_type=f32)
         out_grad = jnp.einsum("tc,td->cd", scaled, branch_rows, preferred_element_type=f32)
         scale_cols = jnp.sum(attended * scaled_grad, axis=0)
@@ -1252,75 +1557,82 @@
             [jnp.sum(gq, axis=0, dtype=f32), jnp.sum(gv, axis=0, dtype=f32)], axis=0
         )
         qkv_grad = jnp.einsum("tc,td->cd", proj_grad, attn_rows, preferred_element_type=f32)
-        qkv_grad, out_grad = share_attn(
-            jnp.concatenate([qkv_grad, out_grad], axis=0).reshape(4, 2, head_width, model_width)
-        )
-        attn_in_grad = plane_scatter(proj_grad, qkv_here, 1, 5)
-        attn_gain_grad = jnp.sum(attn_in_grad * attn_normal, axis=0)
-        attn_bias_grad = jnp.sum(attn_in_grad, axis=0)
-        gradient = middle_grad + norm_back(
-            attn_in_grad, attn_normal, attn_factor, ln_attn_gain[layer]
-        )
-        big[layer] = (qkv_grad, out_grad, first_grad, second_grad)
-        hidden = jnp.stack([first_shift_grad, hidden_gain_grad, hidden_shift_grad])
-        hidden = lax.dynamic_update_slice(
-            jnp.zeros((3, 4, 2, 4, quarter), f32),
-            hidden.reshape(3, 4, 1, 1, quarter),
-            (0, 0, x, quarter_at, 0),
-        )
-        bias_grad = lax.dynamic_update_slice(
-            jnp.zeros((2, 4, 2, 2, head_width), f32),
-            bias_grad.reshape(2, 2, 1, 1, head_width),
-            (0, 2 * core, x, y, 0),
-        )
-        little[layer] = jnp.concatenate(
+        heads_grad = jnp.concatenate([qkv_grad.astype(bf16), out_grad.astype(bf16)], axis=0)
+        heads_grad = heads_grad.reshape(4, 2, head_width, model_width)
+        bias_grad = jnp.transpose(bias_grad.reshape(2, 2, head_width), (1, 0, 2))
+        hidden_grad = jnp.stack([first_shift_grad, hidden_gain_grad, hidden_shift_grad])
+        hidden_grad = jnp.concatenate(
             [
-                hidden.reshape(-1),
-                bias_grad.reshape(-1),
-                attn_gain_grad,
-                attn_bias_grad,
+                jnp.transpose(hidden_grad.reshape(3, 4, quarter), (1, 0, 2)).reshape(4, -1),
+                lax.dynamic_update_slice(
+                    jnp.zeros((4, width), f32), bias_grad.reshape(2, width), (2 * core, 0)
+                ),
+            ],
+            axis=1,
+        ).reshape(4, -1, 128)
+        vector_grads[layer] = jnp.stack(
+            [
                 out_shift_grad,
                 post_gain_grad,
                 post_bias_grad,
                 ffn_gain_grad,
                 ffn_bias_grad,
                 second_shift_grad,
-                scale_grad,
-                jnp.zeros((-heads_all % 128,), f32),
+                jnp.pad(scale_grad, (0, model_width - heads_all)),
             ]
         )
+        sides = [HeadScatter(heads_grad), LineScatter(hidden_grad), RowsGather(first_grad)]
+        if layer == 0:
+            early = [vector_grads[each] for each in range(layers)] + norm_grads
+            sides.append(PlaneSum(jnp.concatenate(early, axis=0)))
+        ((attn_in_grad,), (heads_grad,), (hidden_grad,), (first_grad,), *rest) = run_tasks(
+            ids, PlaneScatter(proj_grad, qkv_here, 0), *sides
+        )
+        pending = (heads_grad, hidden_grad)
+        first_done[layer] = first_grad
+        attn_norm_grads = jnp.stack(
+            [jnp.sum(attn_in_grad * attn_normal, axis=0), jnp.sum(attn_in_grad, axis=0)]
+        )
+        norm_grads.insert(0, attn_norm_grads)
+        gradient = middle_grad + norm_back(
+            attn_in_grad, attn_normal, attn_factor, ln_attn_gain[layer]
+        )
     input_grad = from_plane(gradient.astype(bf16)).astype(f32)
-    stacked = lax.psum(jnp.stack(little), EVERY)
-    shard = 2 * lax.axis_index("z") + x
-    hidden = stacked[:, : 3 * hidden_all].reshape(layers, 3, 8, hidden_here)
-    hidden = lax.dynamic_index_in_dim(hidden, shard, 2, keepdims=False)
-    rest = stacked[:, 3 * hidden_all :]
-    bias_grad = rest[:, : 2 * model_width].reshape(layers, 2, 8, model_width // 8)
-    bias_grad = lax.dynamic_index_in_dim(bias_grad, shard, 2, keepdims=False)
-    rest = rest[:, 2 * model_width :]
-    vectors = [rest[:, i * model_width : (i + 1) * model_width] for i in range(8)]
-    scale_grad = rest[:, 8 * model_width : 8 * model_width + heads_all]
-    weights = [jnp.stack([big[layer][i] for layer in range(layers)]) for i in range(4)]
+    ((vectors,), *got) = run_tasks(
+        ids,
+        PlaneThenLineSum(norm_grads[0], rest[0][0]),
+        RowsGather(pending[0]),
+        RowsGather(pending[1]),
+    )
+    heads_done[0], hidden_done[0] = got[0][0], got[1][0]
+    per_layer = vectors[: 7 * layers].reshape(layers, 7, model_width)
+    later = vectors[7 * layers :].reshape(layers, 2, model_width)[::-1]
+    heads_done = [head_shard(each) for each in heads_done]
+    hidden = jnp.stack(hidden_done).reshape(layers, 4, -1)
+    bias_grad = jnp.sum(hidden[:, :, 3 * quarter :].reshape(layers, 2, 2, 2, head_width), axis=2)
+    bias_grad = jnp.transpose(bias_grad, (0, 2, 1, 3)).reshape(layers, 2, width)
+    hidden = hidden[:, :, : 3 * quarter].reshape(layers, 4, 3, quarter)
+    hidden = jnp.transpose(hidden, (0, 2, 1, 3)).reshape(layers, 3, hidden_here)
     return (
         layer_output,
         input_grad,
-        vectors[0],
-        vectors[1],
-        weights[0],
+        later[:, 0],
+        later[:, 1],
+        jnp.stack([each[0] for each in heads_done]),
         bias_grad,
-        scale_grad,
-        weights[1],
-        vectors[2],
-        vectors[3],
-        vectors[4],
-        vectors[5],
-        vectors[6],
-        weights[2],
+        per_layer[:, 6, :heads_all],
+        jnp.stack([each[1] for each in heads_done]),
+        per_layer[:, 0],
+        per_layer[:, 1],
+        per_layer[:, 2],
+        per_layer[:, 3],
+        per_layer[:, 4],
+        jnp.stack([ffn_shard(each).T for each in first_done]),
         hidden[:, 0],
         hidden[:, 1],
         hidden[:, 2],
-        weights[3],
-        vectors[7],
+        jnp.stack([ffn_shard(each) for each in second_done]),
+        per_layer[:, 5],
     )
 
 

time: 1170 us -> 835 us (0.71)
  waiting for transfers between devices: 314 us -> 35.9 us
  Pallas kernels: 477 us -> 567 us
  blocking collectives: 85.4 us -> 0 us
  other arithmetic: 68.6 us -> 52 us
  between operations: 17 us -> 3.39 us
    psum x1 -> x0, waiting for transfers between devices: 128 us -> none  [plane_device(): stacked = lax.psum(jnp.stack(little), EVERY)]
    pallas_call x20 -> x21, Pallas kernels: 382 us -> 474 us  [run_tasks(): pl.pallas_call(kernel, out_shape=[out for task in tasks for out in task.o...]
    all_gather x10 -> x0, waiting for transfers between devices: 87.9 us -> none  [the longest x4 57.8 us: share_ffn(): return lax.all_gather(mine, ('y', 'core'), axis=0, tiled=True).astype(f32)]
    all_gather x5 -> x0, blocking collectives: 85.4 us -> none  [the longest x2 47.8 us: gather_attn(): stacked = lax.all_gather(qkv, 'z', axis=0)]
    reduce_scatter x6 -> x0, waiting for transfers between devices: 57.8 us -> none  [the longest x2 57.7 us: share_attn(): mine = lax.psum_scatter(stacked, 'z', scatter_dimension=0)]
    ppermute x3, waiting for transfers between devices: 37.8 us -> 11.7 us  [to_plane(): return lax.ppermute(values, EVERY, plane_pairs())]
    ppermute x2, waiting for transfers between devices: 0.01 us -> 24.2 us  [from_plane(): lax.ppermute(values, EVERY, [(target, source) for source, target in plane...]
    unnamed x280 -> x271, local copies, waits for them, and re-layouts: 37.9 us -> 27.3 us
  transfers between devices with their start and end apart: 28 -> 5, of which waited for: 10 -> 3; matrix products, arithmetic and copies ran while one was open for 13% -> 8% of each run, Pallas kernels for 29% -> 29%
where the time goes in v2:
time: 835 us; the launch traced here: 831 us
  Pallas kernels  567 us (68%)
  local copies, waits for them, and re-layouts  79 us (9%)
  matrix products  73.4 us (9%)
  other arithmetic  52 us (6%)
  waiting for transfers between devices  35.9 us (4%)
  starting transfers between devices  19.8 us (2%)
    pallas_call x21, Pallas kernels, run_tasks(): pl.pallas_call(kernel, out_shape=[out for task in tasks for out in task.o...  474 us
    pallas_call x2, Pallas kernels, attend_plane_back(): pl.pallas_call(partial(attend_back_kernel, head_width), grid=(blocks,), o...  47 us
    pallas_call x2, Pallas kernels, attend_plane(): pl.pallas_call(partial(attend_kernel, head_width), grid=(blocks,), out_sh...  46.5 us
    unnamed x271, local copies, waits for them, and re-layouts  27.3 us
    dot_general x2, matrix products, plane_device(): jnp.einsum('td,fd->tf', ffn_rows, first_here[layer], preferred_element_ty...  26.8 us
    ppermute x2, waiting for transfers between devices, from_plane(): lax.ppermute(values, EVERY, [(target, source) for source, target in plane...  24.2 us
  transfers between devices with their start and end apart: 5, of which 3 were waited for; matrix products, arithmetic and copies ran while one was open for 8% of the time, Pallas kernels for 29%

profile of v2, /device:TPU:1, one launch (start us, length us, event | category | flops | bytes accessed | tf_op | source)
XLA Modules:
  0.0 831.0 jit_solution(6488204870633495313)
XLA Ops:
  43.1 31.8 %shard_map.339 = (bf16[2048,1024]{1,0:T(8,128)(2,1)S(1)}, bf16[4,2,64,1024]{3,2,1,0:T(8,128)(2,1)S(1)}, f32[4,2,512]{2,1,0:T(2,128)S(1)}) custom-call(bf16[256,1024]{1,0:T(8,128)(2,1)S(1)} %fusion.21.refs_0_, bf16[4,64,512]{2,1,0:T(8,128)(2,1)S(1)} %pad_maximum_fusion.4.refs_1_, f32[2,512]{1,0:T(2,128)S(1)} %pad_maximum_fusion.13.refs_2_), custom_call_target="tpu_custom_call" | custom-call | tf_op jit(solution)/shard_map/pallas_call | solution.py:624
  82.2 23.3 %shard_map.340 = (f32[2048,128]{1,0:T(8,128)S(1)}, f32[8,1,512]{2,1,0:T(1,128)S(1)}) custom-call(bf16[2048,128]{1,0:T(8,128)(2,1)S(1)} %get-tuple-element.275.q_ref, bf16[2048,128]{1,0:T(8,128)(2,1)S(1)} %get-tuple-element.274.k_ref, bf16[2048,128]{1,0:T(8,128)(2,1)S(1)} %fusion.31.v_ref, s32[2048,1]{1,0:T(8,128)S(1)} %copy.162.dq_ref.dcol_ref, ...), custom_call_target="tpu_custom_call" | custom-call | tf_op jit(solution)/shard_map/pallas_call | solution.py:1161
  106.5 26.7 %shard_map.341 = (f32[256,1024]{1,0:T(8,128)S(1)}, bf16[4,128,1024]{2,1,0:T(8,128)(2,1)S(1)}) custom-call(bf16[2048,128]{1,0:T(8,128)(2,1)S(1)} %multiply_convert_fusion.3.refs_0_, bf16[128,1024]{1,0:T(8,128)(2,1)S(1)} %bitcast.245, bf16[128,1024]{1,0:T(8,128)(2,1)S(1)} %bitcast.256), custom_call_target="tpu_custom_call" | custom-call | tf_op jit(solution)/shard_map/pallas_call | solution.py:624
  135.2 24.6 %shard_map.342 = (bf16[2048,1024]{1,0:T(8,128)(2,1)S(1)}, bf16[4,128,1024]{2,1,0:T(8,128)(2,1)S(1)}) custom-call(bf16[256,1024]{1,0:T(8,128)(2,1)S(1)} %add_convert_fusion.7.refs_0_, bf16[128,1024]{1,0:T(8,128)(2,1)S(1)} %get-tuple-element.349.refs_1_), custom_call_target="tpu_custom_call" | custom-call | tf_op jit(solution)/shard_map/pallas_call | solution.py:624
  159.8 13.2 %fusion.36 = (f32[2048]{0:T(1024)S(1)}, f32[2048]{0:T(1024)S(1)}, f32[2048,512]{1,0:T(8,128)S(1)}, f32[2048,512]{1,0:T(8,128)}, f32[2048,512]{1,0:T(8,128)}) fusion(f32[512]{0:T(512)S(1)} %bitcast.354, bf16[2048,1024]{1,0:T(8,128)(2,1)S(1)} %get-tuple-element.72, bf16[512,1024]{1,0:T(8,128)(2,1)S(1)} %bitcast.258), kind=kOutput, calls=%fused_computation.243 | convolution fusion | flops 2218782720 | bytes 17844224 | tf_op jit(solution)/shard_map/td,fd->tf/dot_general | solution.py:1416
  179.0 28.1 %shard_map.344 = (f32[256,1024]{1,0:T(8,128)S(1)}, bf16[4,2,64,1024]{3,2,1,0:T(8,128)(2,1)S(1)}) custom-call(bf16[2048,512]{1,0:T(8,128)(2,1)S(1)} %add_convert_fusion.3.refs_0_, bf16[512,1024]{1,0:T(8,128)(2,1)S(1)} %bitcast.252, bf16[4,64,512]{2,1,0:T(8,128)(2,1)S(1)} %pad_maximum_fusion.5.refs_2_), custom_call_target="tpu_custom_call" | custom-call | tf_op jit(solution)/shard_map/pallas_call | solution.py:624
  208.0 23.3 %shard_map.345 = (bf16[2048,1024]{1,0:T(8,128)(2,1)S(1)}, bf16[4,128,1024]{2,1,0:T(8,128)(2,1)S(1)}) custom-call(bf16[256,1024]{1,0:T(8,128)(2,1)S(1)} %add_convert_fusion.6.refs_0_, bf16[128,1024]{1,0:T(8,128)(2,1)S(1)} %bitcast.251), custom_call_target="tpu_custom_call" | custom-call | tf_op jit(solution)/shard_map/pallas_call | solution.py:624
  234.0 23.3 %shard_map.346 = (f32[2048,128]{1,0:T(8,128)S(1)}, f32[8,1,512]{2,1,0:T(1,128)S(1)}) custom-call(bf16[2048,128]{1,0:T(8,128)(2,1)S(1)} %get-tuple-element.273.q_ref, bf16[2048,128]{1,0:T(8,128)(2,1)S(1)} %get-tuple-element.272.k_ref, bf16[2048,128]{1,0:T(8,128)(2,1)S(1)} %fusion.29.v_ref, s32[2048,1]{1,0:T(8,128)S(1)} %copy.162.dq_ref.dcol_ref, ...), custom_call_target="tpu_custom_call" | custom-call | tf_op jit(solution)/shard_map/pallas_call | solution.py:1161
  257.4 27.1 %shard_map.347 = (f32[256,1024]{1,0:T(8,128)S(1)}, bf16[4,128,1024]{2,1,0:T(8,128)(2,1)S(1)}) custom-call(bf16[2048,128]{1,0:T(8,128)(2,1)S(1)} %multiply_convert_fusion.2.refs_0_, bf16[128,1024]{1,0:T(8,128)(2,1)S(1)} %bitcast.247, bf16[128,1024]{1,0:T(8,128)(2,1)S(1)} %copy-done.53), custom_call_target="tpu_custom_call" | custom-call | tf_op jit(solution)/shard_map/pallas_call | solution.py:624
  286.6 21.6 %shard_map.348 = bf16[2048,1024]{1,0:T(8,128)(2,1)S(1)} custom-call(bf16[256,1024]{1,0:T(8,128)(2,1)S(1)} %add_convert_fusion.5.refs_0_), custom_call_target="tpu_custom_call" | custom-call | tf_op jit(solution)/shard_map/pallas_call | solution.py:624
  308.3 13.6 %fusion.35 = (f32[2048]{0:T(1024)S(1)}, f32[2048]{0:T(1024)S(1)}, f32[2048,512]{1,0:T(8,128)}, f32[2048,512]{1,0:T(8,128)}, f32[2048,512]{1,0:T(8,128)}) fusion(f32[512]{0:T(512)S(1)} %bitcast.356, bf16[2048,1024]{1,0:T(8,128)(2,1)S(1)} %shard_map.348, bf16[512,1024]{1,0:T(8,128)(2,1)S(1)} %bitcast.261), kind=kOutput, calls=%fused_computation.242 | convolution fusion | flops 2218782720 | bytes 17844224 | tf_op jit(solution)/shard_map/td,fd->tf/dot_general | solution.py:1416
  326.9 22.6 %shard_map.351 = bf16[2048,1024]{1,0:T(8,128)(2,1)S(1)} custom-call(bf16[256,1024]{1,0:T(8,128)(2,1)} %collective-permute-done.3.refs_0_), custom_call_target="tpu_custom_call" | custom-call | tf_op jit(solution)/shard_map/pallas_call | solution.py:624
  376.5 22.8 %shard_map.350 = f32[256,1024]{1,0:T(8,128)S(1)} custom-call(bf16[2048,512]{1,0:T(8,128)(2,1)S(1)} %get-tuple-element.271.refs_0_, bf16[512,1024]{1,0:T(8,128)(2,1)S(1)} %bitcast.264), custom_call_target="tpu_custom_call" | custom-call | tf_op jit(solution)/shard_map/pallas_call | solution.py:624
  406.0 26.5 %shard_map.353 = (f32[256,1024]{1,0:T(8,128)S(1)}, bf16[128,1024]{1,0:T(8,128)(2,1)S(1)}) custom-call(bf16[2048,512]{1,0:T(8,128)(2,1)S(1)} %get-tuple-element.259.refs_0_, bf16[512,1024]{1,0:T(8,128)(2,1)S(1)} %bitcast.262, bf16[4,128,1024]{2,1,0:T(8,128)(2,1)S(1)} %bitcast.266), custom_call_target="tpu_custom_call" | custom-call | tf_op jit(solution)/shard_map/pallas_call | solution.py:624
  437.0 33.2 %shard_map.354 = (bf16[2048,1024]{1,0:T(8,128)(2,1)}, bf16[128,1024]{1,0:T(8,128)(2,1)S(1)}, bf16[4,128,1024]{2,1,0:T(8,128)(2,1)S(1)}) custom-call(bf16[256,1024]{1,0:T(8,128)(2,1)S(1)} %get-tuple-element.250.refs_0_, bf16[4,128,1024]{2,1,0:T(8,128)(2,1)S(1)} %bitcast.249, bf16[128,1024]{1,0:T(8,128)(2,1)S(1)} %get-tuple-element.83.refs_2_), custom_call_target="tpu_custom_call" | custom-call | tf_op jit(solution)/shard_map/pallas_call | solution.py:624
  475.4 23.5 %shard_map.355 = (bf16[2048,128]{1,0:T(8,128)(2,1)S(1)}, bf16[2048,128]{1,0:T(8,128)(2,1)S(1)}, bf16[2048,128]{1,0:T(8,128)(2,1)S(1)}) custom-call(bf16[2048,128]{1,0:T(8,128)(2,1)S(1)} %copy-done.23, bf16[2048,128]{1,0:T(8,128)(2,1)S(1)} %copy-done.21, bf16[2048,128]{1,0:T(8,128)(2,1)S(1)} %copy-done.15, bf16[2048,128]{1,0:T(8,128)(2,1)S(1)} %get-tuple-element.285.do_ref, ...), custom_call_target="tpu_custom_call" | custom-call | tf_op jit(solution)/shard_map/pallas_call | solution.py:1266
  507.7 28.9 %shard_map.356 = (f32[256,1024]{1,0:T(8,128)S(1)}, bf16[4,64,512]{2,1,0:T(8,128)(2,1)S(1)}, f32[4,128]{1,0:T(4,128)S(1)}, bf16[4,128,1024]{2,1,0:T(8,128)(2,1)S(1)}) custom-call(bf16[2048,384]{1,0:T(8,128)(2,1)S(1)} %constant_dynamic-update-slice_fusion.refs_0_, bf16[384,1024]{1,0:T(8,128)(2,1)S(1)} %bitcast.244, bf16[4,2,64,1024]{3,2,1,0:T(8,128)(2,1)S(1)} %bitcast.240, ...), custom_call_target="tpu_custom_call" | custom-call | tf_op jit(solution)/shard_map/pallas_call | solution.py:624
  538.6 29.6 %shard_map.357 = (bf16[2048,1024]{1,0:T(8,128)(2,1)S(1)}, bf16[4,4,64,512]{3,2,1,0:T(8,128)(2,1)S(1)}, f32[4,4,128]{2,1,0:T(4,128)S(1)}) custom-call(bf16[256,1024]{1,0:T(8,128)(2,1)S(1)} %convert_element_type.188.refs_0_, bf16[4,64,512]{2,1,0:T(8,128)(2,1)S(1)} %get-tuple-element.91.refs_1_, f32[4,128]{1,0:T(4,128)S(1)} %get-tuple-element.92.refs_2_), custom_call_target="tpu_custom_call" | custom-call | tf_op jit(solution)/shard_map/pallas_call | solution.py:624
  591.8 23.6 %shard_map.359 = (f32[256,1024]{1,0:T(8,128)S(1)}, bf16[128,1024]{1,0:T(8,128)(2,1)S(1)}) custom-call(bf16[2048,512]{1,0:T(8,128)(2,1)S(1)} %get-tuple-element.256.refs_0_, bf16[512,1024]{1,0:T(8,128)(2,1)S(1)} %bitcast.259, bf16[4,128,1024]{2,1,0:T(8,128)(2,1)S(1)} %bitcast.265), custom_call_target="tpu_custom_call" | custom-call | tf_op jit(solution)/shard_map/pallas_call | solution.py:624
  617.9 33.4 %shard_map.360 = (bf16[2048,1024]{1,0:T(8,128)(2,1)}, bf16[128,1024]{1,0:T(8,128)(2,1)S(1)}, bf16[4,128,1024]{2,1,0:T(8,128)(2,1)S(1)}) custom-call(bf16[256,1024]{1,0:T(8,128)(2,1)S(1)} %get-tuple-element.254.refs_0_, bf16[4,128,1024]{2,1,0:T(8,128)(2,1)S(1)} %bitcast.250, bf16[128,1024]{1,0:T(8,128)(2,1)S(1)} %get-tuple-element.95.refs_2_), custom_call_target="tpu_custom_call" | custom-call | tf_op jit(solution)/shard_map/pallas_call | solution.py:624
  656.0 23.5 %shard_map.361 = (bf16[2048,128]{1,0:T(8,128)(2,1)S(1)}, bf16[2048,128]{1,0:T(8,128)(2,1)S(1)}, bf16[2048,128]{1,0:T(8,128)(2,1)S(1)}) custom-call(bf16[2048,128]{1,0:T(8,128)(2,1)S(1)} %copy-done.19, bf16[2048,128]{1,0:T(8,128)(2,1)S(1)} %copy-done.17, bf16[2048,128]{1,0:T(8,128)(2,1)S(1)} %copy-done.13, bf16[2048,128]{1,0:T(8,128)(2,1)S(1)} %get-tuple-element.283.do_ref, ...), custom_call_target="tpu_custom_call" | custom-call | tf_op jit(solution)/shard_map/pallas_call | solution.py:1266
  692.8 33.7 %shard_map.362 = (f32[256,1024]{1,0:T(8,128)S(1)}, bf16[4,64,512]{2,1,0:T(8,128)(2,1)S(1)}, f32[4,128]{1,0:T(4,128)S(1)}, bf16[4,128,1024]{2,1,0:T(8,128)(2,1)S(1)}, f32[16,1024]{1,0:T(8,128)S(1)}) custom-call(bf16[2048,384]{1,0:T(8,128)(2,1)S(1)} %copy-done.34, bf16[384,1024]{1,0:T(8,128)(2,1)S(1)} %bitcast.242, bf16[4,2,64,1024]{3,2,1,0:T(8,128)(2,1)S(1)} %bitcast.239, ...), custom_call_target="tpu_custom_call" | custom-call | tf_op jit(solution)/shard_map/pallas_call | solution.py:624
  728.5 16.4 %shard_map.363 = (f32[18,1024]{1,0:T(8,128)S(1)}, bf16[4,4,64,512]{3,2,1,0:T(8,128)(2,1)S(1)}, f32[4,4,128]{2,1,0:T(4,128)S(1)}) custom-call(f32[2,1024]{1,0:T(2,128)S(1)} %pad_maximum_fusion.12.refs_0_, f32[16,1024]{1,0:T(8,128)S(1)} %get-tuple-element.103.refs_1_, bf16[4,64,512]{2,1,0:T(8,128)(2,1)S(1)} %get-tuple-element.104.refs_2_, ...), custom_call_target="tpu_custom_call" | custom-call | tf_op jit(solution)/shard_map/pallas_call | solution.py:624
  804.6 19.7 %collective-permute-done.4 = bf16[256,1024]{1,0:T(8,128)(2,1)S(1)} collective-permute-done((bf16[256,1024]{1,0:T(8,128)(2,1)S(1)}, bf16[256,1024]{1,0:T(8,128)(2,1)S(1)}, u32[]{:S(2)}, u32[]{:S(2)}) %collective-permute-start.4) | collective-permute-done | bytes 524320 | tf_op jit(solution)/shard_map/ppermute | solution.py:544
  (496 shorter events, 233.7 us)
Async XLA Ops:
  0.7 41.6 %collective-permute-start = (bf16[256,1024]{1,0:T(8,128)(2,1)}, bf16[256,1024]{1,0:T(8,128)(2,1)S(1)}, u32[]{:S(2)}, u32[]{:S(2)}) collective-permute-start(bf16[256,1024]{1,0:T(8,128)(2,1)} %param.20), channel_id=1, source_target_pairs={{0,0},{1,1},{2,16},{3,17},{4,8},{5,9},{6,24},{7,25},{8,2},{9,3},{1... | collective-permute-start | bytes 1572872 | tf_op jit(solution)/shard_map/ppermute | solution.py:540
  5.4 36.5 %collective-permute-start.1 = (s32[2048]{0:T(1024)}, s32[2048]{0:T(1024)S(1)}, u32[]{:S(2)}, u32[]{:S(2)}) collective-permute-start(s32[2048]{0:T(1024)} %param.21), channel_id=1, source_target_pairs={{0,0},{1,1},{2,16},{3,17},{4,8},{5,9},{6,24},{7,25},{8,2},{9,3},{1... | collective-permute-start | bytes 24584 | tf_op jit(solution)/shard_map/ppermute | solution.py:540
  8.8 318.2 %collective-permute-start.3 = (bf16[256,1024]{1,0:T(8,128)(2,1)}, bf16[256,1024]{1,0:T(8,128)(2,1)}, u32[]{:S(2)}, u32[]{:S(2)}) collective-permute-start(bf16[256,1024]{1,0:T(8,128)(2,1)} %param.22), channel_id=1, source_target_pairs={{0,0},{1,1},{2,16},{3,17},{4,8},{5,9},{6,24},{7,25},{8,2},{9,3},{1... | collective-permute-start | bytes 1572872 | tf_op jit(solution)/shard_map/ppermute | solution.py:540
  21.8 111.9 %copy-start.87 = (f32[1,1024]{1,0:T(1,128)}, f32[1,1024]{1,0:T(1,128)S(1)}, u32[]{:S(2)}) copy-start(f32[1,1024]{1,0:T(1,128)S(1)} %get-tuple-element.320) | copy-start | bytes 12292
  21.8 111.8 %copy-start.91 = (f32[1,1024]{1,0:T(1,128)}, f32[1,1024]{1,0:T(1,128)S(1)}, u32[]{:S(2)}) copy-start(f32[1,1024]{1,0:T(1,128)S(1)} %get-tuple-element.326) | copy-start | bytes 12292
  21.9 113.0 %copy-start.93 = (f32[1,1024]{1,0:T(1,128)}, f32[1,1024]{1,0:T(1,128)S(1)}, u32[]{:S(2)}) copy-start(f32[1,1024]{1,0:T(1,128)S(1)} %get-tuple-element.316) | copy-start | bytes 12292
  29.8 75.8 %copy-start.116 = (f32[128]{0:T(128)}, f32[128]{0:T(128)S(1)}, u32[]{:S(2)}) copy-start(f32[128]{0:T(128)S(1)} %mul.594) | copy-start | bytes 1540
  30.2 227.1 %copy-start.118 = (f32[128]{0:T(128)}, f32[128]{0:T(128)S(1)}, u32[]{:S(2)}) copy-start(f32[128]{0:T(128)S(1)} %mul.629) | copy-start | bytes 1540
  42.5 39.5 %copy-start.97 = (f32[256]{0:T(256)}, f32[256]{0:T(256)S(1)}, u32[]{:S(2)}) copy-start(f32[256]{0:T(256)S(1)} %broadcast_multiply_fusion.17) | copy-start | bytes 3076
  82.2 51.9 %copy-start.71 = (bf16[256,1024]{1,0:T(8,128)(2,1)S(1)}, bf16[256,1024]{1,0:T(8,128)(2,1)}, u32[]{:S(2)}) copy-start(bf16[256,1024]{1,0:T(8,128)(2,1)} %copy-done.70) | copy-start | bytes 1572868
  133.2 39.8 %copy-start.44 = (bf16[4,128,1024]{2,1,0:T(8,128)(2,1)}, bf16[4,128,1024]{2,1,0:T(8,128)(2,1)S(1)}, u32[]{:S(2)}) copy-start(bf16[4,128,1024]{2,1,0:T(8,128)(2,1)S(1)} %get-tuple-element.73) | copy-start | bytes 3145732
  133.3 39.7 %copy-start.95 = (f32[256]{0:T(256)}, f32[256]{0:T(256)S(1)}, u32[]{:S(2)}) copy-start(f32[256]{0:T(256)S(1)} %broadcast_multiply_fusion.16) | copy-start | bytes 3076
  133.6 39.4 %copy-start.101 = (f32[256]{0:T(256)}, f32[256]{0:T(256)S(1)}, u32[]{:S(2)}) copy-start(f32[256]{0:T(256)S(1)} %add_rsqrt_fusion.6) | copy-start | bytes 3076
  134.6 72.7 %copy-start.62 = (f32[256,1024]{1,0:T(8,128)}, f32[256,1024]{1,0:T(8,128)S(1)}, u32[]{:S(2)}) copy-start(f32[256,1024]{1,0:T(8,128)S(1)} %get-tuple-element.270) | copy-start | bytes 3145732
  134.6 38.4 %copy-start.99 = (f32[256]{0:T(256)}, f32[256]{0:T(256)S(1)}, u32[]{:S(2)}) copy-start(f32[256]{0:T(256)S(1)} %broadcast_multiply_fusion.15) | copy-start | bytes 3076
  207.5 78.2 %copy-start.64 = (f32[256,1024]{1,0:T(8,128)}, f32[256,1024]{1,0:T(8,128)S(1)}, u32[]{:S(2)}) copy-start(f32[256,1024]{1,0:T(8,128)S(1)} %get-tuple-element.266) | copy-start | bytes 3145732
  231.4 76.9 %copy-start.48 = (bf16[4,128,1024]{2,1,0:T(8,128)(2,1)}, bf16[4,128,1024]{2,1,0:T(8,128)(2,1)S(1)}, u32[]{:S(2)}) copy-start(bf16[4,128,1024]{2,1,0:T(8,128)(2,1)S(1)} %get-tuple-element.80) | copy-start | bytes 3145732
  234.0 52.1 %copy-start.22 = (bf16[2048,128]{1,0:T(8,128)(2,1)}, bf16[2048,128]{1,0:T(8,128)(2,1)S(1)}, u32[]{:S(2)}) copy-start(bf16[2048,128]{1,0:T(8,128)(2,1)S(1)} %get-tuple-element.273.q_ref) | copy-start | bytes 1572868
  285.3 64.3 %copy-start.50 = (bf16[4,128,1024]{2,1,0:T(8,128)(2,1)}, bf16[4,128,1024]{2,1,0:T(8,128)(2,1)S(1)}, u32[]{:S(2)}) copy-start(bf16[4,128,1024]{2,1,0:T(8,128)(2,1)S(1)} %get-tuple-element.81) | copy-start | bytes 3145732
  436.6 38.7 %copy-start.75 = (f32[256,1024]{1,0:T(8,128)}, f32[256,1024]{1,0:T(8,128)S(1)}, u32[]{:S(2)}) copy-start(f32[256,1024]{1,0:T(8,128)S(1)} %get-tuple-element.260) | copy-start | bytes 3145732
  688.3 38.3 %copy-start.90 = (f32[1,1024]{1,0:T(1,128)S(1)}, f32[1,1024]{1,0:T(1,128)}, u32[]{:S(2)}) copy-start(f32[1,1024]{1,0:T(1,128)} %copy-done.89) | copy-start | bytes 12292
  688.3 38.3 %copy-start.98 = (f32[256]{0:T(256)S(1)}, f32[256]{0:T(256)}, u32[]{:S(2)}) copy-start(f32[256]{0:T(256)} %copy-done.97) | copy-start | bytes 3076
  791.0 33.3 %collective-permute-start.4 = (bf16[256,1024]{1,0:T(8,128)(2,1)S(1)}, bf16[256,1024]{1,0:T(8,128)(2,1)S(1)}, u32[]{:S(2)}, u32[]{:S(2)}) collective-permute-start(bf16[256,1024]{1,0:T(8,128)(2,1)S(1)} %fusion.26), channel_id=1, source_target_pairs={{0,0},{1,1},{16,2},{17,3},{8,4},{9,5},{24,6},{25,7},{2,8},{3,9},{1... | collective-permute-start | bytes 1572872 | tf_op jit(solution)/shard_map/ppermute | solution.py:544
  793.9 36.0 %collective-permute-start.2 = (bf16[256,1024]{1,0:T(8,128)(2,1)}, bf16[256,1024]{1,0:T(8,128)(2,1)S(1)}, u32[]{:S(2)}, u32[]{:S(2)}) collective-permute-start(bf16[256,1024]{1,0:T(8,128)(2,1)} %get-tuple-element.286), channel_id=1, source_target_pairs={{0,0},{1,1},{16,2},{17,3},{8,4},{9,5},{24,6},{25,7},{2,8},{3,9},{1... | collective-permute-start | bytes 1572872 | tf_op jit(solution)/shard_map/ppermute | solution.py:544
  (108 other events, 1665.7 us)
